TPU v7x, 256 devices: a whole 4x4x8 slice. The times are simulated.
256 devices in a mesh: ka: 32 (over z_lo, x, core), an: 8 (over z_hi, y).
Axes of the slice: x: 4, y: 4, z: 8 (z_hi: 2, z_lo: 4; z = z_hi * 4 + z_lo), core: 2. Of those that a mesh axis runs over, the one named last changes fastest.
Arguments:
- out_grad: bfloat16 [1024, 12288], P('ka', 'an'), may hold values from -4 to 4
- saved_input: bfloat16 [1024, 49152], P('an', 'ka'), may hold values from -6 to 6
- down_weight: bfloat16 [49152, 12288], P('ka', 'an'), may hold values from -0.109375 to 0.109375
Outputs:
- weight_grad: bfloat16 [49152, 12288], P('ka', 'an')
- input_grad: bfloat16 [1024, 49152], P('an', 'ka')
All inputs are finite; a program needn't handle non-finite values.
Results may differ from a plain program's by a relative error of at most 0.017.
Values may be sent and summed in bfloat16 or wider, within the bound.
No kernel may reach another device: no remote copies, remote signals or barrier semaphores. Data moves between devices by JAX's collectives and lax.ppermute only.
A program may use at most 64 MiB of HBM per device.

v0:
```python
import math

import jax
import jax.numpy as jnp
from jax import lax
from jax.sharding import PartitionSpec as P

coef = math.sqrt(2.0 / math.pi)


def gelu_value(x):
    u = coef * (x + 0.044715 * x * x * x)
    return 0.5 * x * (1.0 + jnp.tanh(u))


def gelu_slope(x):
    t = jnp.tanh(coef * (x + 0.044715 * x * x * x))
    return 0.5 * (1.0 + t) + 0.5 * x * (1.0 - t * t) * coef * (1.0 + 3.0 * 0.044715 * x * x)


def body(out_grad, saved_input, down_weight):
    inputs = saved_input.astype(jnp.float32)
    gathered = lax.all_gather(saved_input, "an", axis=0, tiled=True)
    activated = gelu_value(gathered.astype(jnp.float32)).astype(jnp.bfloat16)
    grads = lax.all_gather(out_grad, "ka", axis=0, tiled=True)
    weight_grad = lax.dot_general(
        activated, grads, (((0,), (0,)), ((), ())), preferred_element_type=jnp.float32
    ).astype(jnp.bfloat16)
    partial_sums = lax.dot_general(
        grads, down_weight, (((1,), (1,)), ((), ())), preferred_element_type=jnp.float32
    )
    hidden_grad = lax.psum_scatter(
        partial_sums.astype(jnp.bfloat16), "an", scatter_dimension=0, tiled=True
    ).astype(jnp.float32)
    input_grad = (hidden_grad * gelu_slope(inputs)).astype(jnp.bfloat16)
    return (weight_grad, input_grad)


def solution(mesh):
    placed = (P("ka", "an"), P("an", "ka"), P("ka", "an"))
    return jax.shard_map(
        body, mesh=mesh, in_specs=placed, out_specs=(P("ka", "an"), P("an", "ka")), check_vma=False
    )
```

profile of v0, /device:TPU:32, one launch (start us, length us, event | category | flops | bytes accessed | tf_op | source)
XLA Modules:
  0.0 283.9 jit_solution(17153856468296755813)
XLA Ops:
  7.2 0.0 all-gather.5.cloned.1.call-start
  7.2 0.7 all-gather.5.cloned.1.call-update
  7.9 0.0 all-gather.3.cloned.1.call-start
  7.9 0.7 all-gather.3.cloned.1.call-update
  8.6 0.0 reduce-scatter.2.cloned.1.call-start
  8.7 65.0 %all-gather.5.cloned.1.call-done = bf16[1024,1536]{1,0:T(8,128)(2,1)} async-done(((bf16[32,1536]{1,0:T(8,128)(2,1)}), bf16[1024,1536]{1,0:T(8,128)(2,1)}) %all-gather.5.cloned.1.call-update) | async-done | bytes 3145744 | tf_op jit(solution)/shard_map/all_gather | solution.py:25
  73.7 0.0 copy-start.1
  73.7 9.5 %convolution_convert_fusion.1 = bf16[1024,1536]{1,0:T(8,128)(2,1)} fusion(bf16[1024,1536]{1,0:T(8,128)(2,1)} %all-gather.5.cloned.1.call-done, bf16[1536,1536]{1,0:T(8,128)(2,1)} %param.5), kind=kOutput, calls=%fused_computation.11 | convolution fusion | flops 4833411072 | bytes 11010048 | tf_op jit(solution)/shard_map/dot_general | solution.py:29
  83.1 0.0 reduce-scatter.2.cloned.1.call-update
  83.2 0.0 copy-start
  83.2 83.4 %all-gather.3.cloned.1.call-done = bf16[1024,1536]{1,0:T(8,128)(2,1)} async-done(((bf16[128,1536]{1,0:T(8,128)(2,1)}), bf16[1024,1536]{1,0:T(8,128)(2,1)}) %all-gather.3.cloned.1.call-update) | async-done | bytes 3145744 | tf_op jit(solution)/shard_map/all_gather | solution.py:23
  166.6 0.0 copy-done.1
  166.6 11.2 %convolution_convert_fusion = bf16[1536,1536]{1,0:T(8,128)(2,1)} fusion(bf16[1024,1536]{1,0:T(8,128)(2,1)S(1)} %copy-done.1, bf16[1024,1536]{1,0:T(8,128)(2,1)} %all-gather.3.cloned.1.call-done), kind=kOutput, calls=%fused_computation.5 | convolution fusion | flops 4849926144 | bytes 11010048 | tf_op jit(solution)/shard_map/dot_general | solution.py:26
  177.8 97.3 %reduce-scatter.2.cloned.1.call-done = bf16[128,1536]{1,0:T(8,128)(2,1)} async-done(((bf16[1024,1536]{1,0:T(8,128)(2,1)}), bf16[128,1536]{1,0:T(8,128)(2,1)}) %reduce-scatter.2.cloned.1.call-update) | async-done | bytes 393232 | tf_op jit(solution)/shard_map/reduce_scatter | solution.py:32
  275.1 0.0 copy-done
  275.1 2.3 fusion.17
Async XLA Ops:
  7.2 66.5 %all-gather.5.cloned.1.call-start = ((), (), s32[]{:S(2)}) async-start(), calls=%async_computation.2 | async-start | bytes 3244032 | tf_op jit(solution)/shard_map/all_gather | solution.py:25
  7.9 158.7 %all-gather.3.cloned.1.call-start = ((), (), s32[]{:S(2)}) async-start(), calls=%async_computation.1 | async-start | bytes 3538944 | tf_op jit(solution)/shard_map/all_gather | solution.py:23
  8.6 266.5 %reduce-scatter.2.cloned.1.call-start = ((), (), s32[]{:S(2)}) async-start(), calls=%async_computation.3 | async-start | bytes 3538944 | tf_op jit(solution)/shard_map/reduce_scatter | solution.py:32
  73.7 92.9 %copy-start.1 = (bf16[1024,1536]{1,0:T(8,128)(2,1)S(1)}, bf16[1024,1536]{1,0:T(8,128)(2,1)}, u32[]{:S(2)}) copy-start(bf16[1024,1536]{1,0:T(8,128)(2,1)} %all-gather.5.cloned.1.call-done) | copy-start | bytes 9437188
  83.2 191.9 %copy-start = (bf16[128,1536]{1,0:T(8,128)(2,1)S(1)}, bf16[128,1536]{1,0:T(8,128)(2,1)}, u32[]{:S(2)}) copy-start(bf16[128,1536]{1,0:T(8,128)(2,1)} %param.4) | copy-start | bytes 1179652
Sparse Core Ops, SparseCore 0:
  9.9 63.7 all-gather.4
  76.3 90.2 all-gather.2
  170.8 104.2 reduce-scatter.1
where the time goes:
time: 286 us; the launch traced here: 284 us
  waiting for transfers between devices  247 us (86%)
  matrix products  20.7 us (7%)
  between operations  13.8 us (5%)
    reduce_scatter x1, waiting for transfers between devices, body(): lax.psum_scatter(partial_sums.astype(jnp.bfloat16), 'an', scatter_dimensi...  97.3 us
    all_gather x1, waiting for transfers between devices, body(): gathered = lax.all_gather(saved_input, 'an', axis=0, tiled=True)  83.4 us
    all_gather x1, waiting for transfers between devices, body(): grads = lax.all_gather(out_grad, 'ka', axis=0, tiled=True)  65 us
    dot_general x1, matrix products, body(): lax.dot_general(activated, grads, (((0,), (0,)), ((), ())), preferred_ele...  11.2 us
    dot_general x1, matrix products, body(): lax.dot_general(grads, down_weight, (((1,), (1,)), ((), ())), preferred_e...  9.48 us
  transfers between devices with their start and end apart: 3, of which 3 were waited for; matrix products, arithmetic and copies ran while one was open for 7% of the time, Pallas kernels for 0%

commit v1 on v0

v1 whole, which is shorter than its diff:
```python
import math

import jax
import jax.numpy as jnp
from jax import lax
from jax.sharding import Mesh, PartitionSpec as P

coef = math.sqrt(2.0 / math.pi)
AXES = ("zl", "x", "c", "zh", "y")
SIZES = (4, 4, 2, 2, 4)
KA = ("zl", "x", "c")
AN = ("zh", "y")


def gelu_value(x):
    u = coef * (x + 0.044715 * x * x * x)
    return 0.5 * x * (1.0 + jnp.tanh(u))


def gelu_slope(x):
    t = jnp.tanh(coef * (x + 0.044715 * x * x * x))
    return 0.5 * (1.0 + t) + 0.5 * x * (1.0 - t * t) * coef * (1.0 + 3.0 * 0.044715 * x * x)


def send(v, axis, step):
    n = SIZES[AXES.index(axis)]
    return lax.ppermute(v, axis, [(i, (i + step) % n) for i in range(n)])


def place(blocks, me, n):
    out = jnp.zeros((n,) + blocks[0].shape, blocks[0].dtype)
    for k, b in enumerate(blocks):
        out = lax.dynamic_update_index_in_dim(out, b, lax.rem(me + (n - k), n), 0)
    return out


def body(out_grad, saved_input, weight):
    zl, x, c, zh, y = (lax.axis_index(a) for a in AXES)
    rows, width = out_grad.shape
    tok, hidden = saved_input.shape
    other = 1 - zh

    gz = place([out_grad] + [send(out_grad, "zl", k) for k in (1, 2, 3)], zl, 4)

    swapped = send(saved_input, "zh", 1)
    own = [saved_input] + [send(saved_input, "y", k) for k in (1, 2, 3)]
    far = [swapped] + [send(swapped, "y", k) for k in (1, 2, 3)]

    def finish(half):
        part = lax.dynamic_slice_in_dim(gz, 2 * half, 2, 0)
        gx = place([part] + [send(part, "x", k) for k in (1, 2, 3)], x, 4)
        both = place([gx, send(gx, "c", 1)], c, 2)
        return both.transpose(2, 1, 0, 3, 4).reshape(4 * tok, width)

    def partials(g):
        s = lax.dot_general(g, weight, (((1,), (1,)), ((), ())), preferred_element_type=jnp.float32)
        return s.astype(jnp.bfloat16).reshape(4, tok, hidden)

    def reduce_y(p):
        total = lax.dynamic_index_in_dim(p, y, 0, keepdims=False).astype(jnp.float32)
        for k in (1, 2, 3):
            b = lax.dynamic_index_in_dim(p, lax.rem(y + k, 4), 0, keepdims=False)
            total = total + send(b, "y", k).astype(jnp.float32)
        return total

    g_other = finish(other)
    r_other = send(reduce_y(partials(g_other)).astype(jnp.bfloat16), "zh", 1)
    g_mine = finish(zh)
    hidden_grad = reduce_y(partials(g_mine)) + r_other.astype(jnp.float32)
    input_grad = (hidden_grad * gelu_slope(saved_input.astype(jnp.float32))).astype(jnp.bfloat16)

    def act(blocks):
        out = jnp.zeros((4,) + blocks[0].shape, jnp.bfloat16)
        for k, b in enumerate(blocks):
            a = gelu_value(b.astype(jnp.float32)).astype(jnp.bfloat16)
            out = lax.dynamic_update_index_in_dim(out, a, lax.rem(y + (4 - k), 4), 0)
        return out.reshape(4 * tok, hidden)

    activated = jnp.concatenate([act(own), act(far)], 0)
    grads = jnp.concatenate([g_mine, g_other], 0)
    weight_grad = lax.dot_general(
        activated, grads, (((0,), (0,)), ((), ())), preferred_element_type=jnp.float32
    ).astype(jnp.bfloat16)
    return (weight_grad, input_grad)


def solution(mesh):
    fine = Mesh(mesh.devices.reshape(SIZES), AXES)
    return jax.shard_map(
        body,
        mesh=fine,
        in_specs=(P(KA, AN), P(AN, KA), P(KA, AN)),
        out_specs=(P(KA, AN), P(AN, KA)),
        check_vma=False,
    )
```

time: 286 us -> 158 us (0.55)
  the two profiles are of different devices: /device:TPU:32 before, /device:TPU:64 now
where the time goes in v1:
time: 158 us; the launch traced here: 157 us
  waiting for transfers between devices  95.2 us (60%)
  starting transfers between devices  41.2 us (26%)
  matrix products  12 us (8%)
  other arithmetic  4.99 us (3%)
  local copies, waits for them, and re-layouts  3.14 us (2%)
    ppermute x25, waiting for transfers between devices, send(): return lax.ppermute(v, axis, [(i, (i + step) % n) for i in range(n)])  95.2 us
    ppermute x25, starting transfers between devices, send(): return lax.ppermute(v, axis, [(i, (i + step) % n) for i in range(n)])  41.2 us
    dot_general x1, matrix products, body(): lax.dot_general(activated, grads, (((0,), (0,)), ((), ())), preferred_ele...  6.78 us
    dot_general x2, matrix products, partials(): lax.dot_general(g, weight, (((1,), (1,)), ((), ())), preferred_element_ty...  5.26 us
    dynamic_update_slice x8, other arithmetic, act(): out = lax.dynamic_update_index_in_dim(out, a, lax.rem(y + (4 - k), 4), 0)  3.25 us
  transfers between devices with their start and end apart: 25, of which 17 were waited for; matrix products, arithmetic and copies ran while one was open for 12% of the time, Pallas kernels for 0%

profile of v1, /device:TPU:64, one launch (start us, length us, event | category | flops | bytes accessed | tf_op | source)
XLA Modules:
  0.0 157.5 jit_solution(7447746983847716345)
XLA Ops:
  0.6 5.5 %collective-permute-start.3 = (bf16[128,1536]{1,0:T(8,128)(2,1)}, bf16[128,1536]{1,0:T(8,128)(2,1)S(1)}, u32[]{:S(2)}, u32[]{:S(2)}) collective-permute-start(bf16[128,1536]{1,0:T(8,128)(2,1)} %param.4), channel_id=1, source_target_pairs={{0,4},{4,0},{1,5},{5,1},{2,6},{6,2},{3,7},{7,3},{8,12},{12,8},{9,1... | collective-permute-start | bytes 1179656 | tf_op jit(solution)/shard_map/ppermute | solution.py:27
  6.1 1.6 %collective-permute-start = (bf16[128,1536]{1,0:T(8,128)(2,1)}, bf16[128,1536]{1,0:T(8,128)(2,1)}, u32[]{:S(2)}, u32[]{:S(2)}) collective-permute-start(bf16[128,1536]{1,0:T(8,128)(2,1)} %param.4), channel_id=1, source_target_pairs={{0,1},{1,2},{2,3},{3,0},{4,5},{5,6},{6,7},{7,4},{8,9},{9,10},{10,1... | collective-permute-start | bytes 1179656 | tf_op jit(solution)/shard_map/ppermute | solution.py:27
  7.7 2.9 %collective-permute-start.1 = (bf16[128,1536]{1,0:T(8,128)(2,1)}, bf16[128,1536]{1,0:T(8,128)(2,1)S(1)}, u32[]{:S(2)}, u32[]{:S(2)}) collective-permute-start(bf16[128,1536]{1,0:T(8,128)(2,1)} %param.4), channel_id=1, source_target_pairs={{0,2},{1,3},{2,0},{3,1},{4,6},{5,7},{6,4},{7,5},{8,10},{9,11},{10,... | collective-permute-start | bytes 1179656 | tf_op jit(solution)/shard_map/ppermute | solution.py:27
  14.3 12.2 %collective-permute-done.7 = bf16[32,1536]{1,0:T(8,128)(2,1)} collective-permute-done((bf16[32,1536]{1,0:T(8,128)(2,1)}, bf16[32,1536]{1,0:T(8,128)(2,1)}, u32[]{:S(2)}, u32[]{:S(2)}) %collective-permute-start.7) | collective-permute-done | bytes 98336 | tf_op jit(solution)/shard_map/ppermute | solution.py:27
  28.9 3.6 %collective-permute-done.8 = bf16[32,1536]{1,0:T(8,128)(2,1)S(1)} collective-permute-done((bf16[32,1536]{1,0:T(8,128)(2,1)}, bf16[32,1536]{1,0:T(8,128)(2,1)S(1)}, u32[]{:S(2)}, u32[]{:S(2)}) %collective-permute-start.8) | collective-permute-done | bytes 98336 | tf_op jit(solution)/shard_map/ppermute | solution.py:27
  33.1 4.6 %collective-permute-done.9 = bf16[32,1536]{1,0:T(8,128)(2,1)S(1)} collective-permute-done((bf16[32,1536]{1,0:T(8,128)(2,1)}, bf16[32,1536]{1,0:T(8,128)(2,1)S(1)}, u32[]{:S(2)}, u32[]{:S(2)}) %collective-permute-start.9) | collective-permute-done | bytes 98336 | tf_op jit(solution)/shard_map/ppermute | solution.py:27
  37.8 1.6 collective-permute-start.14
  39.5 5.3 %collective-permute-done.14 = bf16[2,32,1536]{2,1,0:T(8,128)(2,1)S(1)} collective-permute-done((bf16[2,32,1536]{2,1,0:T(8,128)(2,1)S(1)}, bf16[2,32,1536]{2,1,0:T(8,128)(2,1)S(1)}, u32[]{:S(2)}, u32[]{:S(2)}) %collective-permute-start.14) | collective-permute-done | bytes 196640 | tf_op jit(solution)/shard_map/ppermute | solution.py:27
  44.8 1.8 %collective-permute-start.15 = (bf16[2,32,1536]{2,1,0:T(8,128)(2,1)S(1)}, bf16[2,32,1536]{2,1,0:T(8,128)(2,1)S(1)}, u32[]{:S(2)}, u32[]{:S(2)}) collective-permute-start(bf16[2,32,1536]{2,1,0:T(8,128)(2,1)S(1)} %get-tuple-element.5), channel_id=1, source_target_pairs={{0,32},{16,48},{32,0},{48,16},{1,33},{17,49},{33,1},{49,17},{2,34}... | collective-permute-start | bytes 589832 | tf_op jit(solution)/shard_map/ppermute | solution.py:27
  46.6 5.3 %collective-permute-done.15 = bf16[2,32,1536]{2,1,0:T(8,128)(2,1)S(1)} collective-permute-done((bf16[2,32,1536]{2,1,0:T(8,128)(2,1)S(1)}, bf16[2,32,1536]{2,1,0:T(8,128)(2,1)S(1)}, u32[]{:S(2)}, u32[]{:S(2)}) %collective-permute-start.15) | collective-permute-done | bytes 196640 | tf_op jit(solution)/shard_map/ppermute | solution.py:27
  52.0 3.0 %collective-permute-start.16 = (bf16[2,32,1536]{2,1,0:T(8,128)(2,1)S(1)}, bf16[2,32,1536]{2,1,0:T(8,128)(2,1)S(1)}, u32[]{:S(2)}, u32[]{:S(2)}) collective-permute-start(bf16[2,32,1536]{2,1,0:T(8,128)(2,1)S(1)} %get-tuple-element.5), channel_id=1, source_target_pairs={{0,48},{16,0},{32,16},{48,32},{1,49},{17,1},{33,17},{49,33},{2,50}... | collective-permute-start | bytes 589832 | tf_op jit(solution)/shard_map/ppermute | solution.py:27
  54.9 3.2 %collective-permute-done.16 = bf16[2,32,1536]{2,1,0:T(8,128)(2,1)S(1)} collective-permute-done((bf16[2,32,1536]{2,1,0:T(8,128)(2,1)S(1)}, bf16[2,32,1536]{2,1,0:T(8,128)(2,1)S(1)}, u32[]{:S(2)}, u32[]{:S(2)}) %collective-permute-start.16) | collective-permute-done | bytes 196640 | tf_op jit(solution)/shard_map/ppermute | solution.py:27
  59.4 7.8 %collective-permute-done.10 = bf16[2,32,1536]{2,1,0:T(8,128)(2,1)S(1)} collective-permute-done((bf16[2,32,1536]{2,1,0:T(8,128)(2,1)S(1)}, bf16[2,32,1536]{2,1,0:T(8,128)(2,1)S(1)}, u32[]{:S(2)}, u32[]{:S(2)}) %collective-permute-start.10) | collective-permute-done | bytes 196640 | tf_op jit(solution)/shard_map/ppermute | solution.py:27
  67.8 6.6 %collective-permute-done.11 = bf16[2,32,1536]{2,1,0:T(8,128)(2,1)S(1)} collective-permute-done((bf16[2,32,1536]{2,1,0:T(8,128)(2,1)S(1)}, bf16[2,32,1536]{2,1,0:T(8,128)(2,1)S(1)}, u32[]{:S(2)}, u32[]{:S(2)}) %collective-permute-start.11) | collective-permute-done | bytes 196640 | tf_op jit(solution)/shard_map/ppermute | solution.py:27
  75.0 5.1 %collective-permute-done.12 = bf16[2,32,1536]{2,1,0:T(8,128)(2,1)S(1)} collective-permute-done((bf16[2,32,1536]{2,1,0:T(8,128)(2,1)S(1)}, bf16[2,32,1536]{2,1,0:T(8,128)(2,1)S(1)}, u32[]{:S(2)}, u32[]{:S(2)}) %collective-permute-start.12) | collective-permute-done | bytes 196640 | tf_op jit(solution)/shard_map/ppermute | solution.py:27
  81.4 1.8 %collective-permute-start.4 = (bf16[128,1536]{1,0:T(8,128)(2,1)S(1)}, bf16[128,1536]{1,0:T(8,128)(2,1)S(1)}, u32[]{:S(2)}, u32[]{:S(2)}) collective-permute-start(bf16[128,1536]{1,0:T(8,128)(2,1)S(1)} %collective-permute-done.3), channel_id=1, source_target_pairs={{0,1},{1,2},{2,3},{3,0},{4,5},{5,6},{6,7},{7,4},{8,9},{9,10},{10,1... | collective-permute-start | bytes 1179656 | tf_op jit(solution)/shard_map/ppermute | solution.py:27
  84.5 3.0 %collective-permute-start.5 = (bf16[128,1536]{1,0:T(8,128)(2,1)S(1)}, bf16[128,1536]{1,0:T(8,128)(2,1)S(1)}, u32[]{:S(2)}, u32[]{:S(2)}) collective-permute-start(bf16[128,1536]{1,0:T(8,128)(2,1)S(1)} %collective-permute-done.3), channel_id=1, source_target_pairs={{0,2},{1,3},{2,0},{3,1},{4,6},{5,7},{6,4},{7,5},{8,10},{9,11},{10,... | collective-permute-start | bytes 1179656 | tf_op jit(solution)/shard_map/ppermute | solution.py:27
  89.5 4.5 %collective-permute-done.4 = bf16[128,1536]{1,0:T(8,128)(2,1)S(1)} collective-permute-done((bf16[128,1536]{1,0:T(8,128)(2,1)S(1)}, bf16[128,1536]{1,0:T(8,128)(2,1)S(1)}, u32[]{:S(2)}, u32[]{:S(2)}) %collective-permute-start.4) | collective-permute-done | bytes 393248 | tf_op jit(solution)/shard_map/ppermute | solution.py:27
  94.2 9.3 %collective-permute-done.5 = bf16[128,1536]{1,0:T(8,128)(2,1)S(1)} collective-permute-done((bf16[128,1536]{1,0:T(8,128)(2,1)S(1)}, bf16[128,1536]{1,0:T(8,128)(2,1)S(1)}, u32[]{:S(2)}, u32[]{:S(2)}) %collective-permute-start.5) | collective-permute-done | bytes 393248 | tf_op jit(solution)/shard_map/ppermute | solution.py:27
  104.8 2.6 %convolution_convert_fusion.1 = bf16[512,1536]{1,0:T(8,128)(2,1)S(1)} fusion(bf16[512,1536]{1,0:T(8,128)(2,1)S(1)} %bitcast.116, bf16[1536,1536]{1,0:T(8,128)(2,1)S(1)} %bitcast.123), kind=kOutput, calls=%fused_computation.7 | convolution fusion | flops 2416705536 | bytes 7864320 | tf_op jit(solution)/shard_map/dot_general | solution.py:56
  107.5 2.7 %collective-permute-start.23 = (bf16[128,1536]{1,0:T(8,128)(2,1)S(1)}, bf16[128,1536]{1,0:T(8,128)(2,1)S(1)}, u32[]{:S(2)}, u32[]{:S(2)}) collective-permute-start(bf16[128,1536]{1,0:T(8,128)(2,1)S(1)} %get-tuple-element.10), channel_id=1, source_target_pairs={{0,3},{1,0},{2,1},{3,2},{4,7},{5,4},{6,5},{7,6},{8,11},{9,8},{10,9... | collective-permute-start | bytes 1179656 | tf_op jit(solution)/shard_map/ppermute | solution.py:27
  110.2 1.5 collective-permute-start.22
  112.2 2.6 %convolution_convert_fusion.2 = bf16[512,1536]{1,0:T(8,128)(2,1)S(1)} fusion(bf16[512,1536]{1,0:T(8,128)(2,1)S(1)} %bitcast.113, bf16[1536,1536]{1,0:T(8,128)(2,1)S(1)} %bitcast.123), kind=kOutput, calls=%fused_computation.8 | convolution fusion | flops 2416705536 | bytes 7864320 | tf_op jit(solution)/shard_map/dot_general | solution.py:56
  115.0 2.9 %collective-permute-start.20 = (bf16[128,1536]{1,0:T(8,128)(2,1)S(1)}, bf16[128,1536]{1,0:T(8,128)(2,1)S(1)}, u32[]{:S(2)}, u32[]{:S(2)}) collective-permute-start(bf16[128,1536]{1,0:T(8,128)(2,1)S(1)} %get-tuple-element.7), channel_id=1, source_target_pairs={{0,3},{1,0},{2,1},{3,2},{4,7},{5,4},{6,5},{7,6},{8,11},{9,8},{10,9... | collective-permute-start | bytes 1179656 | tf_op jit(solution)/shard_map/ppermute | solution.py:27
  118.7 9.3 %collective-permute-done.23 = bf16[128,1536]{1,0:T(8,128)(2,1)S(1)} collective-permute-done((bf16[128,1536]{1,0:T(8,128)(2,1)S(1)}, bf16[128,1536]{1,0:T(8,128)(2,1)S(1)}, u32[]{:S(2)}, u32[]{:S(2)}) %collective-permute-start.23) | collective-permute-done | bytes 393248 | tf_op jit(solution)/shard_map/ppermute | solution.py:27
  128.0 1.6 %collective-permute-start.18 = (bf16[128,1536]{1,0:T(8,128)(2,1)S(1)}, bf16[128,1536]{1,0:T(8,128)(2,1)S(1)}, u32[]{:S(2)}, u32[]{:S(2)}) collective-permute-start(bf16[128,1536]{1,0:T(8,128)(2,1)S(1)} %get-tuple-element.6), channel_id=1, source_target_pairs={{0,1},{1,2},{2,3},{3,0},{4,5},{5,6},{6,7},{7,4},{8,9},{9,10},{10,1... | collective-permute-start | bytes 1179656 | tf_op jit(solution)/shard_map/ppermute | solution.py:27
  129.6 2.6 %collective-permute-done.21 = bf16[128,1536]{1,0:T(8,128)(2,1)S(1)} collective-permute-done((bf16[128,1536]{1,0:T(8,128)(2,1)S(1)}, bf16[128,1536]{1,0:T(8,128)(2,1)S(1)}, u32[]{:S(2)}, u32[]{:S(2)}) %collective-permute-start.21) | collective-permute-done | bytes 393248 | tf_op jit(solution)/shard_map/ppermute | solution.py:27
  134.0 6.8 %convolution_convert_fusion = bf16[1536,1536]{1,0:T(8,128)(2,1)} fusion(bf16[512,1536]{1,0:T(8,128)(2,1)S(1)} %bitcast.112, bf16[512,1536]{1,0:T(8,128)(2,1)S(1)} %bitcast.115, bf16[512,1536]{1,0:T(8,128)(2,1)S(1)} %bitcast.117, bf16[512,1536]{1,0:T(8,128)(2,1)S(1)} %bitcast.114), kind=kOutput, calls=%fused_computation | convolution fusion | flops 4846780416 | bytes 11010048 | tf_op jit(solution)/shard_map/dot_general | solution.py:81
  140.8 3.3 %collective-permute-done.20 = bf16[128,1536]{1,0:T(8,128)(2,1)S(1)} collective-permute-done((bf16[128,1536]{1,0:T(8,128)(2,1)S(1)}, bf16[128,1536]{1,0:T(8,128)(2,1)S(1)}, u32[]{:S(2)}, u32[]{:S(2)}) %collective-permute-start.20) | collective-permute-done | bytes 393248 | tf_op jit(solution)/shard_map/ppermute | solution.py:27
  144.1 3.7 %collective-permute-done.18 = bf16[128,1536]{1,0:T(8,128)(2,1)S(1)} collective-permute-done((bf16[128,1536]{1,0:T(8,128)(2,1)S(1)}, bf16[128,1536]{1,0:T(8,128)(2,1)S(1)}, u32[]{:S(2)}, u32[]{:S(2)}) %collective-permute-start.18) | collective-permute-done | bytes 393248 | tf_op jit(solution)/shard_map/ppermute | solution.py:27
  147.8 8.2 %collective-permute-done.24 = bf16[128,1536]{1,0:T(8,128)(2,1)S(1)} collective-permute-done((bf16[128,1536]{1,0:T(8,128)(2,1)S(1)}, bf16[128,1536]{1,0:T(8,128)(2,1)S(1)}, u32[]{:S(2)}, u32[]{:S(2)}) %collective-permute-start.24) | collective-permute-done | bytes 393248 | tf_op jit(solution)/shard_map/ppermute | solution.py:27
  156.0 1.5 fusion.13
  (63 shorter events, 18.5 us)
Async XLA Ops:
  0.6 12.5 %copy-start = (bf16[128,1536]{1,0:T(8,128)(2,1)S(1)}, bf16[128,1536]{1,0:T(8,128)(2,1)}, u32[]{:S(2)}) copy-start(bf16[128,1536]{1,0:T(8,128)(2,1)} %param.4) | copy-start | bytes 1179652
  0.6 79.7 %collective-permute-start.3 = (bf16[128,1536]{1,0:T(8,128)(2,1)}, bf16[128,1536]{1,0:T(8,128)(2,1)S(1)}, u32[]{:S(2)}, u32[]{:S(2)}) collective-permute-start(bf16[128,1536]{1,0:T(8,128)(2,1)} %param.4), channel_id=1, source_target_pairs={{0,4},{4,0},{1,5},{5,1},{2,6},{6,2},{3,7},{7,3},{8,12},{12,8},{9,1... | collective-permute-start | bytes 1179656 | tf_op jit(solution)/shard_map/ppermute | solution.py:27
  6.1 75.3 %collective-permute-start = (bf16[128,1536]{1,0:T(8,128)(2,1)}, bf16[128,1536]{1,0:T(8,128)(2,1)}, u32[]{:S(2)}, u32[]{:S(2)}) collective-permute-start(bf16[128,1536]{1,0:T(8,128)(2,1)} %param.4), channel_id=1, source_target_pairs={{0,1},{1,2},{2,3},{3,0},{4,5},{5,6},{6,7},{7,4},{8,9},{9,10},{10,1... | collective-permute-start | bytes 1179656 | tf_op jit(solution)/shard_map/ppermute | solution.py:27
  7.7 76.8 %collective-permute-start.1 = (bf16[128,1536]{1,0:T(8,128)(2,1)}, bf16[128,1536]{1,0:T(8,128)(2,1)S(1)}, u32[]{:S(2)}, u32[]{:S(2)}) collective-permute-start(bf16[128,1536]{1,0:T(8,128)(2,1)} %param.4), channel_id=1, source_target_pairs={{0,2},{1,3},{2,0},{3,1},{4,6},{5,7},{6,4},{7,5},{8,10},{9,11},{10,... | collective-permute-start | bytes 1179656 | tf_op jit(solution)/shard_map/ppermute | solution.py:27
  10.6 77.2 %collective-permute-start.2 = (bf16[128,1536]{1,0:T(8,128)(2,1)}, bf16[128,1536]{1,0:T(8,128)(2,1)S(1)}, u32[]{:S(2)}, u32[]{:S(2)}) collective-permute-start(bf16[128,1536]{1,0:T(8,128)(2,1)} %param.4), channel_id=1, source_target_pairs={{0,3},{1,0},{2,1},{3,2},{4,7},{5,4},{6,5},{7,6},{8,11},{9,8},{10,9... | collective-permute-start | bytes 1179656 | tf_op jit(solution)/shard_map/ppermute | solution.py:27
  11.9 14.6 %collective-permute-start.7 = (bf16[32,1536]{1,0:T(8,128)(2,1)}, bf16[32,1536]{1,0:T(8,128)(2,1)}, u32[]{:S(2)}, u32[]{:S(2)}) collective-permute-start(bf16[32,1536]{1,0:T(8,128)(2,1)} %param.3), channel_id=1, source_target_pairs={{0,64},{64,128},{128,192},{192,0},{1,65},{65,129},{129,193},{193,1... | collective-permute-start | bytes 294920 | tf_op jit(solution)/shard_map/ppermute | solution.py:27
  26.6 5.9 %collective-permute-start.8 = (bf16[32,1536]{1,0:T(8,128)(2,1)}, bf16[32,1536]{1,0:T(8,128)(2,1)S(1)}, u32[]{:S(2)}, u32[]{:S(2)}) collective-permute-start(bf16[32,1536]{1,0:T(8,128)(2,1)} %param.3), channel_id=1, source_target_pairs={{0,128},{64,192},{128,0},{192,64},{1,129},{65,193},{129,1},{193,65... | collective-permute-start | bytes 294920 | tf_op jit(solution)/shard_map/ppermute | solution.py:27
  32.5 5.2 %collective-permute-start.9 = (bf16[32,1536]{1,0:T(8,128)(2,1)}, bf16[32,1536]{1,0:T(8,128)(2,1)S(1)}, u32[]{:S(2)}, u32[]{:S(2)}) collective-permute-start(bf16[32,1536]{1,0:T(8,128)(2,1)} %param.3), channel_id=1, source_target_pairs={{0,192},{64,0},{128,64},{192,128},{1,193},{65,1},{129,65},{193,129... | collective-permute-start | bytes 294920 | tf_op jit(solution)/shard_map/ppermute | solution.py:27
  37.8 7.0 %collective-permute-start.14 = (bf16[2,32,1536]{2,1,0:T(8,128)(2,1)S(1)}, bf16[2,32,1536]{2,1,0:T(8,128)(2,1)S(1)}, u32[]{:S(2)}, u32[]{:S(2)}) collective-permute-start(bf16[2,32,1536]{2,1,0:T(8,128)(2,1)S(1)} %get-tuple-element.5), channel_id=1, source_target_pairs={{0,16},{16,32},{32,48},{48,0},{1,17},{17,33},{33,49},{49,1},{2,18}... | collective-permute-start | bytes 589832 | tf_op jit(solution)/shard_map/ppermute | solution.py:27
  44.8 7.2 %collective-permute-start.15 = (bf16[2,32,1536]{2,1,0:T(8,128)(2,1)S(1)}, bf16[2,32,1536]{2,1,0:T(8,128)(2,1)S(1)}, u32[]{:S(2)}, u32[]{:S(2)}) collective-permute-start(bf16[2,32,1536]{2,1,0:T(8,128)(2,1)S(1)} %get-tuple-element.5), channel_id=1, source_target_pairs={{0,32},{16,48},{32,0},{48,16},{1,33},{17,49},{33,1},{49,17},{2,34}... | collective-permute-start | bytes 589832 | tf_op jit(solution)/shard_map/ppermute | solution.py:27
  52.0 6.1 %collective-permute-start.16 = (bf16[2,32,1536]{2,1,0:T(8,128)(2,1)S(1)}, bf16[2,32,1536]{2,1,0:T(8,128)(2,1)S(1)}, u32[]{:S(2)}, u32[]{:S(2)}) collective-permute-start(bf16[2,32,1536]{2,1,0:T(8,128)(2,1)S(1)} %get-tuple-element.5), channel_id=1, source_target_pairs={{0,48},{16,0},{32,16},{48,32},{1,49},{17,1},{33,17},{49,33},{2,50}... | collective-permute-start | bytes 589832 | tf_op jit(solution)/shard_map/ppermute | solution.py:27
  58.1 9.1 %collective-permute-start.10 = (bf16[2,32,1536]{2,1,0:T(8,128)(2,1)S(1)}, bf16[2,32,1536]{2,1,0:T(8,128)(2,1)S(1)}, u32[]{:S(2)}, u32[]{:S(2)}) collective-permute-start(bf16[2,32,1536]{2,1,0:T(8,128)(2,1)S(1)} %get-tuple-element.3), channel_id=1, source_target_pairs={{0,16},{16,32},{32,48},{48,0},{1,17},{17,33},{33,49},{49,1},{2,18}... | collective-permute-start | bytes 589832 | tf_op jit(solution)/shard_map/ppermute | solution.py:27
  59.4 45.4 %slice-start = ((s8[4718592]{0:T(1024)(128)(4,1)}), s8[4194304]{0:T(1024)(128)(4,1)S(1)}, s32[]{:S(2)}) async-start(s8[4718592]{0:T(1024)(128)(4,1)} %bitcast.122), calls=%async_computation | async-start | bytes 8388608
  67.2 7.2 %collective-permute-start.11 = (bf16[2,32,1536]{2,1,0:T(8,128)(2,1)S(1)}, bf16[2,32,1536]{2,1,0:T(8,128)(2,1)S(1)}, u32[]{:S(2)}, u32[]{:S(2)}) collective-permute-start(bf16[2,32,1536]{2,1,0:T(8,128)(2,1)S(1)} %get-tuple-element.3), channel_id=1, source_target_pairs={{0,32},{16,48},{32,0},{48,16},{1,33},{17,49},{33,1},{49,17},{2,34}... | collective-permute-start | bytes 589832 | tf_op jit(solution)/shard_map/ppermute | solution.py:27
  74.4 5.7 %collective-permute-start.12 = (bf16[2,32,1536]{2,1,0:T(8,128)(2,1)S(1)}, bf16[2,32,1536]{2,1,0:T(8,128)(2,1)S(1)}, u32[]{:S(2)}, u32[]{:S(2)}) collective-permute-start(bf16[2,32,1536]{2,1,0:T(8,128)(2,1)S(1)} %get-tuple-element.3), channel_id=1, source_target_pairs={{0,48},{16,0},{32,16},{48,32},{1,49},{17,1},{33,17},{49,33},{2,50}... | collective-permute-start | bytes 589832 | tf_op jit(solution)/shard_map/ppermute | solution.py:27
  80.1 24.6 %collective-permute-start.17 = (bf16[4,2,32,1536]{3,2,0,1:T(8,128)(2,1)S(1)}, bf16[4,2,32,1536]{3,2,0,1:T(8,128)(2,1)S(1)}, u32[]{:S(2)}, u32[]{:S(2)}) collective-permute-start(bf16[4,2,32,1536]{3,2,0,1:T(8,128)(2,1)S(1)} %bitcast_dynamic-update-slice_fusion.4), channel_id=1, source_target_pairs={{0,8},{8,0},{1,9},{9,1},{2,10},{10,2},{3,11},{11,3},{4,12},{12,4},... | collective-permute-start | bytes 2359304 | tf_op jit(solution)/shard_map/ppermute | solution.py:27
  80.3 24.4 %slice-start.1 = ((s8[4718592]{0:T(1024)(128)(4,1)}), s8[524288]{0:T(1024)(128)(4,1)S(1)}, s32[]{:S(2)}) async-start(s8[4718592]{0:T(1024)(128)(4,1)} %bitcast.122), calls=%async_computation.1 | async-start | bytes 1048576
  80.4 31.8 %collective-permute-start.13 = (bf16[4,2,32,1536]{3,2,0,1:T(8,128)(2,1)S(1)}, bf16[4,2,32,1536]{3,2,0,1:T(8,128)(2,1)S(1)}, u32[]{:S(2)}, u32[]{:S(2)}) collective-permute-start(bf16[4,2,32,1536]{3,2,0,1:T(8,128)(2,1)S(1)} %bitcast_dynamic-update-slice_fusion.10), channel_id=1, source_target_pairs={{0,8},{8,0},{1,9},{9,1},{2,10},{10,2},{3,11},{11,3},{4,12},{12,4},... | collective-permute-start | bytes 2359304 | tf_op jit(solution)/shard_map/ppermute | solution.py:27
  81.4 12.6 %collective-permute-start.4 = (bf16[128,1536]{1,0:T(8,128)(2,1)S(1)}, bf16[128,1536]{1,0:T(8,128)(2,1)S(1)}, u32[]{:S(2)}, u32[]{:S(2)}) collective-permute-start(bf16[128,1536]{1,0:T(8,128)(2,1)S(1)} %collective-permute-done.3), channel_id=1, source_target_pairs={{0,1},{1,2},{2,3},{3,0},{4,5},{5,6},{6,7},{7,4},{8,9},{9,10},{10,1... | collective-permute-start | bytes 1179656 | tf_op jit(solution)/shard_map/ppermute | solution.py:27
  84.5 19.0 %collective-permute-start.5 = (bf16[128,1536]{1,0:T(8,128)(2,1)S(1)}, bf16[128,1536]{1,0:T(8,128)(2,1)S(1)}, u32[]{:S(2)}, u32[]{:S(2)}) collective-permute-start(bf16[128,1536]{1,0:T(8,128)(2,1)S(1)} %collective-permute-done.3), channel_id=1, source_target_pairs={{0,2},{1,3},{2,0},{3,1},{4,6},{5,7},{6,4},{7,5},{8,10},{9,11},{10,... | collective-permute-start | bytes 1179656 | tf_op jit(solution)/shard_map/ppermute | solution.py:27
  87.8 16.6 %collective-permute-start.6 = (bf16[128,1536]{1,0:T(8,128)(2,1)S(1)}, bf16[128,1536]{1,0:T(8,128)(2,1)S(1)}, u32[]{:S(2)}, u32[]{:S(2)}) collective-permute-start(bf16[128,1536]{1,0:T(8,128)(2,1)S(1)} %collective-permute-done.3), channel_id=1, source_target_pairs={{0,3},{1,0},{2,1},{3,2},{4,7},{5,4},{6,5},{7,6},{8,11},{9,8},{10,9... | collective-permute-start | bytes 1179656 | tf_op jit(solution)/shard_map/ppermute | solution.py:27
  107.5 20.5 %collective-permute-start.23 = (bf16[128,1536]{1,0:T(8,128)(2,1)S(1)}, bf16[128,1536]{1,0:T(8,128)(2,1)S(1)}, u32[]{:S(2)}, u32[]{:S(2)}) collective-permute-start(bf16[128,1536]{1,0:T(8,128)(2,1)S(1)} %get-tuple-element.10), channel_id=1, source_target_pairs={{0,3},{1,0},{2,1},{3,2},{4,7},{5,4},{6,5},{7,6},{8,11},{9,8},{10,9... | collective-permute-start | bytes 1179656 | tf_op jit(solution)/shard_map/ppermute | solution.py:27
  110.2 19.4 %collective-permute-start.22 = (bf16[128,1536]{1,0:T(8,128)(2,1)S(1)}, bf16[128,1536]{1,0:T(8,128)(2,1)S(1)}, u32[]{:S(2)}, u32[]{:S(2)}) collective-permute-start(bf16[128,1536]{1,0:T(8,128)(2,1)S(1)} %get-tuple-element.11), channel_id=1, source_target_pairs={{0,2},{1,3},{2,0},{3,1},{4,6},{5,7},{6,4},{7,5},{8,10},{9,11},{10,... | collective-permute-start | bytes 1179656 | tf_op jit(solution)/shard_map/ppermute | solution.py:27
  111.7 20.5 %collective-permute-start.21 = (bf16[128,1536]{1,0:T(8,128)(2,1)S(1)}, bf16[128,1536]{1,0:T(8,128)(2,1)S(1)}, u32[]{:S(2)}, u32[]{:S(2)}) collective-permute-start(bf16[128,1536]{1,0:T(8,128)(2,1)S(1)} %get-tuple-element.9), channel_id=1, source_target_pairs={{0,1},{1,2},{2,3},{3,0},{4,5},{5,6},{6,7},{7,4},{8,9},{9,10},{10,1... | collective-permute-start | bytes 1179656 | tf_op jit(solution)/shard_map/ppermute | solution.py:27
  115.0 29.1 %collective-permute-start.20 = (bf16[128,1536]{1,0:T(8,128)(2,1)S(1)}, bf16[128,1536]{1,0:T(8,128)(2,1)S(1)}, u32[]{:S(2)}, u32[]{:S(2)}) collective-permute-start(bf16[128,1536]{1,0:T(8,128)(2,1)S(1)} %get-tuple-element.7), channel_id=1, source_target_pairs={{0,3},{1,0},{2,1},{3,2},{4,7},{5,4},{6,5},{7,6},{8,11},{9,8},{10,9... | collective-permute-start | bytes 1179656 | tf_op jit(solution)/shard_map/ppermute | solution.py:27
  117.9 26.2 %collective-permute-start.19 = (bf16[128,1536]{1,0:T(8,128)(2,1)S(1)}, bf16[128,1536]{1,0:T(8,128)(2,1)S(1)}, u32[]{:S(2)}, u32[]{:S(2)}) collective-permute-start(bf16[128,1536]{1,0:T(8,128)(2,1)S(1)} %get-tuple-element.8), channel_id=1, source_target_pairs={{0,2},{1,3},{2,0},{3,1},{4,6},{5,7},{6,4},{7,5},{8,10},{9,11},{10,... | collective-permute-start | bytes 1179656 | tf_op jit(solution)/shard_map/ppermute | solution.py:27
  128.0 19.8 %collective-permute-start.18 = (bf16[128,1536]{1,0:T(8,128)(2,1)S(1)}, bf16[128,1536]{1,0:T(8,128)(2,1)S(1)}, u32[]{:S(2)}, u32[]{:S(2)}) collective-permute-start(bf16[128,1536]{1,0:T(8,128)(2,1)S(1)} %get-tuple-element.6), channel_id=1, source_target_pairs={{0,1},{1,2},{2,3},{3,0},{4,5},{5,6},{6,7},{7,4},{8,9},{9,10},{10,1... | collective-permute-start | bytes 1179656 | tf_op jit(solution)/shard_map/ppermute | solution.py:27
  132.5 23.4 %collective-permute-start.24 = (bf16[128,1536]{1,0:T(8,128)(2,1)S(1)}, bf16[128,1536]{1,0:T(8,128)(2,1)S(1)}, u32[]{:S(2)}, u32[]{:S(2)}) collective-permute-start(bf16[128,1536]{1,0:T(8,128)(2,1)S(1)} %fusion.54), channel_id=1, source_target_pairs={{0,4},{4,0},{1,5},{5,1},{2,6},{6,2},{3,7},{7,3},{8,12},{12,8},{9,1... | collective-permute-start | bytes 1179656 | tf_op jit(solution)/shard_map/ppermute | solution.py:27

commit v2 on v1

v2 whole, which is shorter than its diff:
```python
import math

import jax
import jax.numpy as jnp
from jax import lax
from jax.sharding import Mesh, PartitionSpec as P

coef = math.sqrt(2.0 / math.pi)
AXES = ("zl", "x", "c", "zh", "y")
SIZES = (4, 4, 2, 2, 4)
KA = ("zl", "x", "c")
AN = ("zh", "y")


def gelu_value(x):
    u = coef * (x + 0.044715 * x * x * x)
    return 0.5 * x * (1.0 + jnp.tanh(u))


def gelu_slope(x):
    t = jnp.tanh(coef * (x + 0.044715 * x * x * x))
    return 0.5 * (1.0 + t) + 0.5 * x * (1.0 - t * t) * coef * (1.0 + 3.0 * 0.044715 * x * x)


def send(v, axis, step):
    n = SIZES[AXES.index(axis)]
    return lax.ppermute(v, axis, [(i, (i + step) % n) for i in range(n)])


def place(blocks, me, n):
    out = jnp.zeros((n,) + blocks[0].shape, blocks[0].dtype)
    for k, b in enumerate(blocks):
        out = lax.dynamic_update_index_in_dim(out, b, lax.rem(me + (n - k), n), 0)
    return out


def spread(v, axis, n):
    return lax.all_to_all(jnp.broadcast_to(v[None], (n,) + v.shape), axis, 0, 0, tiled=True)


def after(v, *done):
    return lax.optimization_barrier((v,) + done)[0]


def body(out_grad, saved_input, weight):
    zl, x, c, zh, y = (lax.axis_index(a) for a in AXES)
    rows, width = out_grad.shape
    tok, hidden = saved_input.shape

    def for_y(p, k):
        return lax.dynamic_index_in_dim(p, lax.rem(y + k, 4), 0, keepdims=False)

    def add_up(p, received):
        total = lax.dynamic_index_in_dim(p, y, 0, keepdims=False).astype(jnp.float32)
        for b in received:
            total = total + b.astype(jnp.float32)
        return total

    def act(blocks):
        out = jnp.zeros((4,) + blocks[0].shape, jnp.bfloat16)
        for k, b in enumerate(blocks):
            a = gelu_value(b.astype(jnp.float32)).astype(jnp.bfloat16)
            out = lax.dynamic_update_index_in_dim(out, a, lax.rem(y + (4 - k), 4), 0)
        return out.reshape(4 * tok, hidden)

    gz = place([out_grad] + [send(out_grad, "zl", k) for k in (1, 2, 3)], zl, 4)
    own1, own3 = (send(saved_input, "y", k) for k in (1, 3))

    gz = after(gz, own1, own3)
    gx = place([gz] + [send(gz, "x", k) for k in (1, 2, 3)], x, 4)
    swapped = send(after(saved_input, own1), "zh", 1)
    own2 = send(after(saved_input, own1), "y", 2)

    gc = place([gx, send(after(gx, swapped, own2), "c", 1)], c, 2)
    far1, far3 = (send(swapped, "y", k) for k in (1, 3))
    grads = gc.transpose(2, 1, 0, 3, 4).reshape(8 * tok, width)
    sums = lax.dot_general(grads, weight, (((1,), (1,)), ((), ())), preferred_element_type=jnp.float32)
    sums = sums.astype(jnp.bfloat16).reshape(2, 4, tok, hidden)
    p_other = lax.dynamic_index_in_dim(sums, 1 - zh, 0, keepdims=False)
    p_mine = lax.dynamic_index_in_dim(sums, zh, 0, keepdims=False)

    p_ready = after(p_other, far1, far3)
    r_other = [send(for_y(p_ready, k), "y", k) for k in (1, 3, 2)]
    far2 = send(after(swapped, far1), "y", 2)

    p_ready = after(p_mine, far2, r_other[0])
    r_mine = [send(for_y(p_ready, k), "y", k) for k in (1, 3, 2)]
    s_other = send(add_up(p_other, r_other).astype(jnp.bfloat16), "zh", 1)

    own = [after(b, gz) for b in (saved_input, own1, own2, own3)]
    far = [after(b, sums) for b in (swapped, far1, far2, far3)]
    low = lax.dynamic_update_index_in_dim(jnp.zeros((2, 4 * tok, hidden), jnp.bfloat16), act(own), zh, 0)
    activated = lax.dynamic_update_index_in_dim(low, act(far), 1 - zh, 0).reshape(8 * tok, hidden)
    weight_grad = lax.dot_general(
        activated, grads, (((0,), (0,)), ((), ())), preferred_element_type=jnp.float32
    ).astype(jnp.bfloat16)
    hidden_grad = add_up(p_mine, r_mine) + s_other.astype(jnp.float32)
    input_grad = (hidden_grad * gelu_slope(saved_input.astype(jnp.float32))).astype(jnp.bfloat16)
    return (weight_grad, input_grad)


def solution(mesh):
    fine = Mesh(mesh.devices.reshape(SIZES), AXES)
    return jax.shard_map(
        body,
        mesh=fine,
        in_specs=(P(KA, AN), P(AN, KA), P(KA, AN)),
        out_specs=(P(KA, AN), P(AN, KA)),
        check_vma=False,
    )
```

time: 158 us -> 111 us (0.70)
  waiting for transfers between devices: 95.2 us -> 45.7 us
  matrix products: 12 us -> 14.4 us
    ppermute x25 -> x21, waiting for transfers between devices: 95.2 us -> 45.7 us  [send(): return lax.ppermute(v, axis, [(i, (i + step) % n) for i in range(n)])]
    dot_general x2 -> x1, matrix products: 5.26 us -> 7.64 us  [body(): lax.dot_general(grads, weight, (((1,), (1,)), ((), ())), preferred_elemen...]
    ppermute x25 -> x21, starting transfers between devices: 41.2 us -> 40.3 us  [send(): return lax.ppermute(v, axis, [(i, (i + step) % n) for i in range(n)])]
    dynamic_update_slice x8 -> x7, other arithmetic: 3.25 us -> 3.29 us  [act(): out = lax.dynamic_update_index_in_dim(out, a, lax.rem(y + (4 - k), 4), 0)]
  transfers between devices with their start and end apart: 25 -> 21, of which waited for: 17 -> 9; matrix products, arithmetic and copies ran while one was open for 12% -> 19% of each run, Pallas kernels for 0% -> 0%
where the time goes in v2:
time: 111 us
  waiting for transfers between devices  45.7 us (41%)
  starting transfers between devices  40.3 us (36%)
  matrix products  14.4 us (13%)
  other arithmetic  5.03 us (5%)
  local copies, waits for them, and re-layouts  4.46 us (4%)
    ppermute x21, waiting for transfers between devices, send(): return lax.ppermute(v, axis, [(i, (i + step) % n) for i in range(n)])  45.7 us
    ppermute x21, starting transfers between devices, send(): return lax.ppermute(v, axis, [(i, (i + step) % n) for i in range(n)])  40.3 us
    dot_general x1, matrix products, body(): lax.dot_general(grads, weight, (((1,), (1,)), ((), ())), preferred_elemen...  7.64 us
    dot_general x1, matrix products, body(): lax.dot_general(activated, grads, (((0,), (0,)), ((), ())), preferred_ele...  6.78 us
    dynamic_update_slice x7, other arithmetic, act(): out = lax.dynamic_update_index_in_dim(out, a, lax.rem(y + (4 - k), 4), 0)  3.29 us
  transfers between devices with their start and end apart: 21, of which 9 were waited for; matrix products, arithmetic and copies ran while one was open for 19% of the time, Pallas kernels for 0%

profile of v2, /device:TPU:64, one launch (start us, length us, event | category | flops | bytes accessed | tf_op | source)
XLA Modules:
  0.0 110.9 jit_solution(11892543745306962160)
XLA Ops:
  0.6 2.0 %collective-permute-start = (bf16[32,1536]{1,0:T(8,128)(2,1)}, bf16[32,1536]{1,0:T(8,128)(2,1)S(1)}, u32[]{:S(2)}, u32[]{:S(2)}) collective-permute-start(bf16[32,1536]{1,0:T(8,128)(2,1)} %param.3), channel_id=1, source_target_pairs={{0,64},{64,128},{128,192},{192,0},{1,65},{65,129},{129,193},{193,1... | collective-permute-start | bytes 294920 | tf_op jit(solution)/shard_map/ppermute | solution.py:27
  2.6 2.4 %collective-permute-start.2 = (bf16[32,1536]{1,0:T(8,128)(2,1)}, bf16[32,1536]{1,0:T(8,128)(2,1)S(1)}, u32[]{:S(2)}, u32[]{:S(2)}) collective-permute-start(bf16[32,1536]{1,0:T(8,128)(2,1)} %param.3), channel_id=1, source_target_pairs={{0,192},{64,0},{128,64},{192,128},{1,193},{65,1},{129,65},{193,129... | collective-permute-start | bytes 294920 | tf_op jit(solution)/shard_map/ppermute | solution.py:27
  5.0 0.7 collective-permute-start.3
  5.8 2.5 %collective-permute-start.4 = (bf16[128,1536]{1,0:T(8,128)(2,1)}, bf16[128,1536]{1,0:T(8,128)(2,1)S(1)}, u32[]{:S(2)}, u32[]{:S(2)}) collective-permute-start(bf16[128,1536]{1,0:T(8,128)(2,1)} %param.4), channel_id=1, source_target_pairs={{0,3},{1,0},{2,1},{3,2},{4,7},{5,4},{6,5},{7,6},{8,11},{9,8},{10,9... | collective-permute-start | bytes 1179656 | tf_op jit(solution)/shard_map/ppermute | solution.py:27
  8.3 0.9 bitcast_dynamic-update-slice_fusion.11
  9.2 1.3 %collective-permute-done = bf16[32,1536]{1,0:T(8,128)(2,1)S(1)} collective-permute-done((bf16[32,1536]{1,0:T(8,128)(2,1)}, bf16[32,1536]{1,0:T(8,128)(2,1)S(1)}, u32[]{:S(2)}, u32[]{:S(2)}) %collective-permute-start) | collective-permute-done | bytes 98336 | tf_op jit(solution)/shard_map/ppermute | solution.py:27
  10.5 0.6 collective-permute-done.2
  11.1 4.8 %collective-permute-done.3 = bf16[128,1536]{1,0:T(8,128)(2,1)S(1)} collective-permute-done((bf16[128,1536]{1,0:T(8,128)(2,1)}, bf16[128,1536]{1,0:T(8,128)(2,1)S(1)}, u32[]{:S(2)}, u32[]{:S(2)}) %collective-permute-start.3) | collective-permute-done | bytes 393248 | tf_op jit(solution)/shard_map/ppermute | solution.py:27
  16.0 1.5 %collective-permute-start.7 = (bf16[4,32,1536]{2,1,0:T(8,128)(2,1)S(1)}, bf16[4,32,1536]{2,1,0:T(8,128)(2,1)S(1)}, u32[]{:S(2)}, u32[]{:S(2)}) collective-permute-start(bf16[4,32,1536]{2,1,0:T(8,128)(2,1)S(1)} %bitcast_dynamic-update-slice_fusion.8), channel_id=1, source_target_pairs={{0,16},{16,32},{32,48},{48,0},{1,17},{17,33},{33,49},{49,1},{2,18}... | collective-permute-start | bytes 1179656 | tf_op jit(solution)/shard_map/ppermute | solution.py:27
  17.5 2.7 %collective-permute-start.8 = (bf16[4,32,1536]{2,1,0:T(8,128)(2,1)S(1)}, bf16[4,32,1536]{2,1,0:T(8,128)(2,1)S(1)}, u32[]{:S(2)}, u32[]{:S(2)}) collective-permute-start(bf16[4,32,1536]{2,1,0:T(8,128)(2,1)S(1)} %bitcast_dynamic-update-slice_fusion.8), channel_id=1, source_target_pairs={{0,32},{16,48},{32,0},{48,16},{1,33},{17,49},{33,1},{49,17},{2,34}... | collective-permute-start | bytes 1179656 | tf_op jit(solution)/shard_map/ppermute | solution.py:27
  20.3 1.4 %collective-permute-start.9 = (bf16[4,32,1536]{2,1,0:T(8,128)(2,1)S(1)}, bf16[4,32,1536]{2,1,0:T(8,128)(2,1)S(1)}, u32[]{:S(2)}, u32[]{:S(2)}) collective-permute-start(bf16[4,32,1536]{2,1,0:T(8,128)(2,1)S(1)} %bitcast_dynamic-update-slice_fusion.8), channel_id=1, source_target_pairs={{0,48},{16,0},{32,16},{48,32},{1,49},{17,1},{33,17},{49,33},{2,50}... | collective-permute-start | bytes 1179656 | tf_op jit(solution)/shard_map/ppermute | solution.py:27
  21.7 6.0 %collective-permute-start.6 = (bf16[128,1536]{1,0:T(8,128)(2,1)}, bf16[128,1536]{1,0:T(8,128)(2,1)S(1)}, u32[]{:S(2)}, u32[]{:S(2)}) collective-permute-start(bf16[128,1536]{1,0:T(8,128)(2,1)} %param.4), channel_id=1, source_target_pairs={{0,4},{4,0},{1,5},{5,1},{2,6},{6,2},{3,7},{7,3},{8,12},{12,8},{9,1... | collective-permute-start | bytes 1179656 | tf_op jit(solution)/shard_map/ppermute | solution.py:27
  27.7 2.8 %collective-permute-start.5 = (bf16[128,1536]{1,0:T(8,128)(2,1)}, bf16[128,1536]{1,0:T(8,128)(2,1)}, u32[]{:S(2)}, u32[]{:S(2)}) collective-permute-start(bf16[128,1536]{1,0:T(8,128)(2,1)} %param.4), channel_id=1, source_target_pairs={{0,2},{1,3},{2,0},{3,1},{4,6},{5,7},{6,4},{7,5},{8,10},{9,11},{10,... | collective-permute-start | bytes 1179656 | tf_op jit(solution)/shard_map/ppermute | solution.py:27
  30.8 5.3 %collective-permute-done.8 = bf16[4,32,1536]{2,1,0:T(8,128)(2,1)S(1)} collective-permute-done((bf16[4,32,1536]{2,1,0:T(8,128)(2,1)S(1)}, bf16[4,32,1536]{2,1,0:T(8,128)(2,1)S(1)}, u32[]{:S(2)}, u32[]{:S(2)}) %collective-permute-start.8) | collective-permute-done | bytes 393248 | tf_op jit(solution)/shard_map/ppermute | solution.py:27
  36.2 6.8 %collective-permute-done.6 = bf16[128,1536]{1,0:T(8,128)(2,1)S(1)} collective-permute-done((bf16[128,1536]{1,0:T(8,128)(2,1)}, bf16[128,1536]{1,0:T(8,128)(2,1)S(1)}, u32[]{:S(2)}, u32[]{:S(2)}) %collective-permute-start.6) | collective-permute-done | bytes 393248 | tf_op jit(solution)/shard_map/ppermute | solution.py:27
  43.0 0.7 copy-done.5
  45.0 1.3 %collective-permute-start.11 = (bf16[128,1536]{1,0:T(8,128)(2,1)S(1)}, bf16[128,1536]{1,0:T(8,128)(2,1)S(1)}, u32[]{:S(2)}, u32[]{:S(2)}) collective-permute-start(bf16[128,1536]{1,0:T(8,128)(2,1)S(1)} %copy-done.6), channel_id=1, source_target_pairs={{0,1},{1,2},{2,3},{3,0},{4,5},{5,6},{6,7},{7,4},{8,9},{9,10},{10,1... | collective-permute-start | bytes 1179656 | tf_op jit(solution)/shard_map/ppermute | solution.py:27
  46.3 2.1 %collective-permute-start.13 = (bf16[128,1536]{1,0:T(8,128)(2,1)S(1)}, bf16[128,1536]{1,0:T(8,128)(2,1)S(1)}, u32[]{:S(2)}, u32[]{:S(2)}) collective-permute-start(bf16[128,1536]{1,0:T(8,128)(2,1)S(1)} %copy-done.6), channel_id=1, source_target_pairs={{0,3},{1,0},{2,1},{3,2},{4,7},{5,4},{6,5},{7,6},{8,11},{9,8},{10,9... | collective-permute-start | bytes 1179656 | tf_op jit(solution)/shard_map/ppermute | solution.py:27
  48.9 8.9 %collective-permute-done.11 = bf16[128,1536]{1,0:T(8,128)(2,1)S(1)} collective-permute-done((bf16[128,1536]{1,0:T(8,128)(2,1)S(1)}, bf16[128,1536]{1,0:T(8,128)(2,1)S(1)}, u32[]{:S(2)}, u32[]{:S(2)}) %collective-permute-start.11) | collective-permute-done | bytes 393248 | tf_op jit(solution)/shard_map/ppermute | solution.py:27
  57.8 1.3 %collective-permute-start.12 = (bf16[128,1536]{1,0:T(8,128)(2,1)S(1)}, bf16[128,1536]{1,0:T(8,128)(2,1)S(1)}, u32[]{:S(2)}, u32[]{:S(2)}) collective-permute-start(bf16[128,1536]{1,0:T(8,128)(2,1)S(1)} %copy-done.6), channel_id=1, source_target_pairs={{0,2},{1,3},{2,0},{3,1},{4,6},{5,7},{6,4},{7,5},{8,10},{9,11},{10,... | collective-permute-start | bytes 1179656 | tf_op jit(solution)/shard_map/ppermute | solution.py:27
  59.3 7.6 %convolution_convert_fusion.1 = bf16[1024,1536]{1,0:T(8,128)(2,1)S(1)} fusion(bf16[1024,1536]{1,0:T(8,128)(2,1)S(1)} %bitcast.103, bf16[1536,1536]{1,0:T(8,128)(2,1)} %param.5), kind=kOutput, calls=%fused_computation.1 | convolution fusion | flops 4833411072 | bytes 11010048 | tf_op jit(solution)/shard_map/dot_general | solution.py:77
  67.3 1.0 collective-permute-start.14
  68.3 2.3 %collective-permute-start.18 = (bf16[128,1536]{1,0:T(8,128)(2,1)S(1)}, bf16[128,1536]{1,0:T(8,128)(2,1)S(1)}, u32[]{:S(2)}, u32[]{:S(2)}) collective-permute-start(bf16[128,1536]{1,0:T(8,128)(2,1)S(1)} %get-tuple-element.37), channel_id=1, source_target_pairs={{0,3},{1,0},{2,1},{3,2},{4,7},{5,4},{6,5},{7,6},{8,11},{9,8},{10,9... | collective-permute-start | bytes 1179656 | tf_op jit(solution)/shard_map/ppermute | solution.py:27
  70.6 1.0 collective-permute-start.19
  72.4 1.6 %fusion.58 = (bf16[4,128,1536]{2,1,0:T(8,128)(2,1)S(1)}, bf16[4,128,1536]{2,1,0:T(8,128)(2,1)S(1)}) fusion(bf16[4,128,1536]{2,1,0:T(8,128)(2,1)S(1)} %fusion.60, s32[]{:T(128)S(6)} %select_n.83, bf16[128,1536]{1,0:T(8,128)(2,1)S(1)} %collective-permute-done.12, bf16[4,128,1536]{2,1,0:T(8,128)(2,1)S(1)} %fusion.68, bf16[128,1536]{1,0:T(8,128)(2,1)} %collective-permute-done.5), kind=kLoop, calls=%fused_computation.115 | loop fusion | flops 3932160 | bytes 1572868 | tf_op jit(solution)/shard_map/jit(dynamic_update_index_in_dim)/dynamic_update_slice | solution.py:63
  75.1 11.7 %collective-permute-done.14 = bf16[128,1536]{1,0:T(8,128)(2,1)S(1)} collective-permute-done((bf16[128,1536]{1,0:T(8,128)(2,1)S(1)}, bf16[128,1536]{1,0:T(8,128)(2,1)S(1)}, u32[]{:S(2)}, u32[]{:S(2)}) %collective-permute-start.14) | collective-permute-done | bytes 393248 | tf_op jit(solution)/shard_map/ppermute | solution.py:27
  87.0 3.2 %collective-permute-start.16 = (bf16[128,1536]{1,0:T(8,128)(2,1)S(1)}, bf16[128,1536]{1,0:T(8,128)(2,1)S(1)}, u32[]{:S(2)}, u32[]{:S(2)}) collective-permute-start(bf16[128,1536]{1,0:T(8,128)(2,1)S(1)} %get-tuple-element.34), channel_id=1, source_target_pairs={{0,3},{1,0},{2,1},{3,2},{4,7},{5,4},{6,5},{7,6},{8,11},{9,8},{10,9... | collective-permute-start | bytes 1179656 | tf_op jit(solution)/shard_map/ppermute | solution.py:27
  90.4 5.9 %collective-permute-start.20 = (bf16[128,1536]{1,0:T(8,128)(2,1)S(1)}, bf16[128,1536]{1,0:T(8,128)(2,1)S(1)}, u32[]{:S(2)}, u32[]{:S(2)}) collective-permute-start(bf16[128,1536]{1,0:T(8,128)(2,1)S(1)} %fusion.51), channel_id=1, source_target_pairs={{0,4},{4,0},{1,5},{5,1},{2,6},{6,2},{3,7},{7,3},{8,12},{12,8},{9,1... | collective-permute-start | bytes 1179656 | tf_op jit(solution)/shard_map/ppermute | solution.py:27
  96.3 6.8 %convolution_convert_fusion = bf16[1536,1536]{1,0:T(8,128)(2,1)} fusion(bf16[1024,1536]{1,0:T(8,128)(2,1)S(1)} %bitcast.102, bf16[1024,1536]{1,0:T(8,128)(2,1)S(1)} %bitcast.104), kind=kOutput, calls=%fused_computation | convolution fusion | flops 4834197504 | bytes 11010048 | tf_op jit(solution)/shard_map/dot_general | solution.py:94
  103.1 1.2 %collective-permute-done.15 = bf16[128,1536]{1,0:T(8,128)(2,1)S(1)} collective-permute-done((bf16[128,1536]{1,0:T(8,128)(2,1)S(1)}, bf16[128,1536]{1,0:T(8,128)(2,1)S(1)}, u32[]{:S(2)}, u32[]{:S(2)}) %collective-permute-start.15) | collective-permute-done | bytes 393248 | tf_op jit(solution)/shard_map/ppermute | solution.py:27
  104.4 5.0 %collective-permute-done.20 = bf16[128,1536]{1,0:T(8,128)(2,1)S(1)} collective-permute-done((bf16[128,1536]{1,0:T(8,128)(2,1)S(1)}, bf16[128,1536]{1,0:T(8,128)(2,1)S(1)}, u32[]{:S(2)}, u32[]{:S(2)}) %collective-permute-start.20) | collective-permute-done | bytes 393248 | tf_op jit(solution)/shard_map/ppermute | solution.py:27
  109.4 1.5 %fusion.47 = bf16[128,1536]{1,0:T(8,128)(2,1)} fusion(bf16[128,1536]{1,0:T(8,128)(2,1)S(1)} %copy-done, bf16[128,1536]{1,0:T(8,128)(2,1)S(1)} %collective-permute-done.20, bf16[128,1536]{1,0:T(8,128)(2,1)S(1)} %collective-permute-done.17, bf16[128,1536]{1,0:T(8,128)(2,1)S(1)} %collective-permute-done.16, bf16[128,1536]{1,0:T(8,128)(2,1)S(1)} %collective-permute-done.15, ...), kind=kLoop, calls=%fused_computation.102 | loop fusion | flops 5701632 | bytes 2752520 | tf_op jit(solution)/shard_map/convert_element_type | solution.py:98
  (56 shorter events, 4.9 us)
Async XLA Ops:
  0.6 9.8 %collective-permute-start = (bf16[32,1536]{1,0:T(8,128)(2,1)}, bf16[32,1536]{1,0:T(8,128)(2,1)S(1)}, u32[]{:S(2)}, u32[]{:S(2)}) collective-permute-start(bf16[32,1536]{1,0:T(8,128)(2,1)} %param.3), channel_id=1, source_target_pairs={{0,64},{64,128},{128,192},{192,0},{1,65},{65,129},{129,193},{193,1... | collective-permute-start | bytes 294920 | tf_op jit(solution)/shard_map/ppermute | solution.py:27
  2.6 7.9 %collective-permute-start.1 = (bf16[32,1536]{1,0:T(8,128)(2,1)}, bf16[32,1536]{1,0:T(8,128)(2,1)S(1)}, u32[]{:S(2)}, u32[]{:S(2)}) collective-permute-start(bf16[32,1536]{1,0:T(8,128)(2,1)} %param.3), channel_id=1, source_target_pairs={{0,128},{64,192},{128,0},{192,64},{1,129},{65,193},{129,1},{193,65... | collective-permute-start | bytes 294920 | tf_op jit(solution)/shard_map/ppermute | solution.py:27
  2.6 8.5 %collective-permute-start.2 = (bf16[32,1536]{1,0:T(8,128)(2,1)}, bf16[32,1536]{1,0:T(8,128)(2,1)S(1)}, u32[]{:S(2)}, u32[]{:S(2)}) collective-permute-start(bf16[32,1536]{1,0:T(8,128)(2,1)} %param.3), channel_id=1, source_target_pairs={{0,192},{64,0},{128,64},{192,128},{1,193},{65,1},{129,65},{193,129... | collective-permute-start | bytes 294920 | tf_op jit(solution)/shard_map/ppermute | solution.py:27
  5.0 10.9 %collective-permute-start.3 = (bf16[128,1536]{1,0:T(8,128)(2,1)}, bf16[128,1536]{1,0:T(8,128)(2,1)S(1)}, u32[]{:S(2)}, u32[]{:S(2)}) collective-permute-start(bf16[128,1536]{1,0:T(8,128)(2,1)} %param.4), channel_id=1, source_target_pairs={{0,1},{1,2},{2,3},{3,0},{4,5},{5,6},{6,7},{7,4},{8,9},{9,10},{10,1... | collective-permute-start | bytes 1179656 | tf_op jit(solution)/shard_map/ppermute | solution.py:27
  5.8 10.2 %collective-permute-start.4 = (bf16[128,1536]{1,0:T(8,128)(2,1)}, bf16[128,1536]{1,0:T(8,128)(2,1)S(1)}, u32[]{:S(2)}, u32[]{:S(2)}) collective-permute-start(bf16[128,1536]{1,0:T(8,128)(2,1)} %param.4), channel_id=1, source_target_pairs={{0,3},{1,0},{2,1},{3,2},{4,7},{5,4},{6,5},{7,6},{8,11},{9,8},{10,9... | collective-permute-start | bytes 1179656 | tf_op jit(solution)/shard_map/ppermute | solution.py:27
  16.0 11.7 %copy-start.3 = (bf16[128,1536]{1,0:T(8,128)(2,1)}, bf16[128,1536]{1,0:T(8,128)(2,1)S(1)}, u32[]{:S(2)}) copy-start(bf16[128,1536]{1,0:T(8,128)(2,1)S(1)} %collective-permute-done.3) | copy-start | bytes 1179652
  16.0 11.7 %copy-start.1 = (bf16[128,1536]{1,0:T(8,128)(2,1)}, bf16[128,1536]{1,0:T(8,128)(2,1)S(1)}, u32[]{:S(2)}) copy-start(bf16[128,1536]{1,0:T(8,128)(2,1)S(1)} %collective-permute-done.4) | copy-start | bytes 1179652
  16.0 14.8 %collective-permute-start.7 = (bf16[4,32,1536]{2,1,0:T(8,128)(2,1)S(1)}, bf16[4,32,1536]{2,1,0:T(8,128)(2,1)S(1)}, u32[]{:S(2)}, u32[]{:S(2)}) collective-permute-start(bf16[4,32,1536]{2,1,0:T(8,128)(2,1)S(1)} %bitcast_dynamic-update-slice_fusion.8), channel_id=1, source_target_pairs={{0,16},{16,32},{32,48},{48,0},{1,17},{17,33},{33,49},{49,1},{2,18}... | collective-permute-start | bytes 1179656 | tf_op jit(solution)/shard_map/ppermute | solution.py:27
  17.5 18.6 %collective-permute-start.8 = (bf16[4,32,1536]{2,1,0:T(8,128)(2,1)S(1)}, bf16[4,32,1536]{2,1,0:T(8,128)(2,1)S(1)}, u32[]{:S(2)}, u32[]{:S(2)}) collective-permute-start(bf16[4,32,1536]{2,1,0:T(8,128)(2,1)S(1)} %bitcast_dynamic-update-slice_fusion.8), channel_id=1, source_target_pairs={{0,32},{16,48},{32,0},{48,16},{1,33},{17,49},{33,1},{49,17},{2,34}... | collective-permute-start | bytes 1179656 | tf_op jit(solution)/shard_map/ppermute | solution.py:27
  20.3 15.9 %collective-permute-start.9 = (bf16[4,32,1536]{2,1,0:T(8,128)(2,1)S(1)}, bf16[4,32,1536]{2,1,0:T(8,128)(2,1)S(1)}, u32[]{:S(2)}, u32[]{:S(2)}) collective-permute-start(bf16[4,32,1536]{2,1,0:T(8,128)(2,1)S(1)} %bitcast_dynamic-update-slice_fusion.8), channel_id=1, source_target_pairs={{0,48},{16,0},{32,16},{48,32},{1,49},{17,1},{33,17},{49,33},{2,50}... | collective-permute-start | bytes 1179656 | tf_op jit(solution)/shard_map/ppermute | solution.py:27
  21.7 21.3 %collective-permute-start.6 = (bf16[128,1536]{1,0:T(8,128)(2,1)}, bf16[128,1536]{1,0:T(8,128)(2,1)S(1)}, u32[]{:S(2)}, u32[]{:S(2)}) collective-permute-start(bf16[128,1536]{1,0:T(8,128)(2,1)} %param.4), channel_id=1, source_target_pairs={{0,4},{4,0},{1,5},{5,1},{2,6},{6,2},{3,7},{7,3},{8,12},{12,8},{9,1... | collective-permute-start | bytes 1179656 | tf_op jit(solution)/shard_map/ppermute | solution.py:27
  27.7 16.0 %collective-permute-start.5 = (bf16[128,1536]{1,0:T(8,128)(2,1)}, bf16[128,1536]{1,0:T(8,128)(2,1)}, u32[]{:S(2)}, u32[]{:S(2)}) collective-permute-start(bf16[128,1536]{1,0:T(8,128)(2,1)} %param.4), channel_id=1, source_target_pairs={{0,2},{1,3},{2,0},{3,1},{4,6},{5,7},{6,4},{7,5},{8,10},{9,11},{10,... | collective-permute-start | bytes 1179656 | tf_op jit(solution)/shard_map/ppermute | solution.py:27
  30.8 13.1 %copy-start = (bf16[128,1536]{1,0:T(8,128)(2,1)S(1)}, bf16[128,1536]{1,0:T(8,128)(2,1)}, u32[]{:S(2)}) copy-start(bf16[128,1536]{1,0:T(8,128)(2,1)} %param.4) | copy-start | bytes 1179652
  43.0 0.7 copy-start.5
  43.7 15.4 %collective-permute-start.10 = (bf16[4,4,32,1536]{3,2,0,1:T(8,128)(2,1)S(1)}, bf16[4,4,32,1536]{3,2,0,1:T(8,128)(2,1)S(1)}, u32[]{:S(2)}, u32[]{:S(2)}) collective-permute-start(bf16[4,4,32,1536]{3,2,0,1:T(8,128)(2,1)S(1)} %bitcast_dynamic-update-slice_fusion.7), channel_id=1, source_target_pairs={{0,8},{8,0},{1,9},{9,1},{2,10},{10,2},{3,11},{11,3},{4,12},{12,4},... | collective-permute-start | bytes 4718600 | tf_op jit(solution)/shard_map/ppermute | solution.py:27
  43.7 1.0 copy-start.4
  43.7 1.3 %copy-start.6 = (bf16[128,1536]{1,0:T(8,128)(2,1)S(1)}, bf16[128,1536]{1,0:T(8,128)(2,1)}, u32[]{:S(2)}) copy-start(bf16[128,1536]{1,0:T(8,128)(2,1)} %copy-done.5) | copy-start | bytes 1179652
  45.0 12.8 %collective-permute-start.11 = (bf16[128,1536]{1,0:T(8,128)(2,1)S(1)}, bf16[128,1536]{1,0:T(8,128)(2,1)S(1)}, u32[]{:S(2)}, u32[]{:S(2)}) collective-permute-start(bf16[128,1536]{1,0:T(8,128)(2,1)S(1)} %copy-done.6), channel_id=1, source_target_pairs={{0,1},{1,2},{2,3},{3,0},{4,5},{5,6},{6,7},{7,4},{8,9},{9,10},{10,1... | collective-permute-start | bytes 1179656 | tf_op jit(solution)/shard_map/ppermute | solution.py:27
  46.3 20.9 %collective-permute-start.13 = (bf16[128,1536]{1,0:T(8,128)(2,1)S(1)}, bf16[128,1536]{1,0:T(8,128)(2,1)S(1)}, u32[]{:S(2)}, u32[]{:S(2)}) collective-permute-start(bf16[128,1536]{1,0:T(8,128)(2,1)S(1)} %copy-done.6), channel_id=1, source_target_pairs={{0,3},{1,0},{2,1},{3,2},{4,7},{5,4},{6,5},{7,6},{8,11},{9,8},{10,9... | collective-permute-start | bytes 1179656 | tf_op jit(solution)/shard_map/ppermute | solution.py:27
  57.8 13.8 %collective-permute-start.12 = (bf16[128,1536]{1,0:T(8,128)(2,1)S(1)}, bf16[128,1536]{1,0:T(8,128)(2,1)S(1)}, u32[]{:S(2)}, u32[]{:S(2)}) collective-permute-start(bf16[128,1536]{1,0:T(8,128)(2,1)S(1)} %copy-done.6), channel_id=1, source_target_pairs={{0,2},{1,3},{2,0},{3,1},{4,6},{5,7},{6,4},{7,5},{8,10},{9,11},{10,... | collective-permute-start | bytes 1179656 | tf_op jit(solution)/shard_map/ppermute | solution.py:27
  67.3 19.5 %collective-permute-start.14 = (bf16[128,1536]{1,0:T(8,128)(2,1)S(1)}, bf16[128,1536]{1,0:T(8,128)(2,1)S(1)}, u32[]{:S(2)}, u32[]{:S(2)}) collective-permute-start(bf16[128,1536]{1,0:T(8,128)(2,1)S(1)} %get-tuple-element.35), channel_id=1, source_target_pairs={{0,1},{1,2},{2,3},{3,0},{4,5},{5,6},{6,7},{7,4},{8,9},{9,10},{10,1... | collective-permute-start | bytes 1179656 | tf_op jit(solution)/shard_map/ppermute | solution.py:27
  68.3 21.9 %collective-permute-start.18 = (bf16[128,1536]{1,0:T(8,128)(2,1)S(1)}, bf16[128,1536]{1,0:T(8,128)(2,1)S(1)}, u32[]{:S(2)}, u32[]{:S(2)}) collective-permute-start(bf16[128,1536]{1,0:T(8,128)(2,1)S(1)} %get-tuple-element.37), channel_id=1, source_target_pairs={{0,3},{1,0},{2,1},{3,2},{4,7},{5,4},{6,5},{7,6},{8,11},{9,8},{10,9... | collective-permute-start | bytes 1179656 | tf_op jit(solution)/shard_map/ppermute | solution.py:27
  70.6 19.6 %collective-permute-start.19 = (bf16[128,1536]{1,0:T(8,128)(2,1)S(1)}, bf16[128,1536]{1,0:T(8,128)(2,1)S(1)}, u32[]{:S(2)}, u32[]{:S(2)}) collective-permute-start(bf16[128,1536]{1,0:T(8,128)(2,1)S(1)} %get-tuple-element.36), channel_id=1, source_target_pairs={{0,2},{1,3},{2,0},{3,1},{4,6},{5,7},{6,4},{7,5},{8,10},{9,11},{10,... | collective-permute-start | bytes 1179656 | tf_op jit(solution)/shard_map/ppermute | solution.py:27
  72.1 2.2 %copy-start.2 = (bf16[128,1536]{1,0:T(8,128)(2,1)S(1)}, bf16[128,1536]{1,0:T(8,128)(2,1)}, u32[]{:S(2)}) copy-start(bf16[128,1536]{1,0:T(8,128)(2,1)} %copy-done.1) | copy-start | bytes 1179652
  86.9 17.5 %collective-permute-start.15 = (bf16[128,1536]{1,0:T(8,128)(2,1)S(1)}, bf16[128,1536]{1,0:T(8,128)(2,1)S(1)}, u32[]{:S(2)}, u32[]{:S(2)}) collective-permute-start(bf16[128,1536]{1,0:T(8,128)(2,1)S(1)} %get-tuple-element.32), channel_id=1, source_target_pairs={{0,1},{1,2},{2,3},{3,0},{4,5},{5,6},{6,7},{7,4},{8,9},{9,10},{10,1... | collective-permute-start | bytes 1179656 | tf_op jit(solution)/shard_map/ppermute | solution.py:27
  87.0 17.4 %collective-permute-start.16 = (bf16[128,1536]{1,0:T(8,128)(2,1)S(1)}, bf16[128,1536]{1,0:T(8,128)(2,1)S(1)}, u32[]{:S(2)}, u32[]{:S(2)}) collective-permute-start(bf16[128,1536]{1,0:T(8,128)(2,1)S(1)} %get-tuple-element.34), channel_id=1, source_target_pairs={{0,3},{1,0},{2,1},{3,2},{4,7},{5,4},{6,5},{7,6},{8,11},{9,8},{10,9... | collective-permute-start | bytes 1179656 | tf_op jit(solution)/shard_map/ppermute | solution.py:27
  90.2 14.2 %collective-permute-start.17 = (bf16[128,1536]{1,0:T(8,128)(2,1)S(1)}, bf16[128,1536]{1,0:T(8,128)(2,1)S(1)}, u32[]{:S(2)}, u32[]{:S(2)}) collective-permute-start(bf16[128,1536]{1,0:T(8,128)(2,1)S(1)} %get-tuple-element.33), channel_id=1, source_target_pairs={{0,2},{1,3},{2,0},{3,1},{4,6},{5,7},{6,4},{7,5},{8,10},{9,11},{10,... | collective-permute-start | bytes 1179656 | tf_op jit(solution)/shard_map/ppermute | solution.py:27
  90.4 18.9 %collective-permute-start.20 = (bf16[128,1536]{1,0:T(8,128)(2,1)S(1)}, bf16[128,1536]{1,0:T(8,128)(2,1)S(1)}, u32[]{:S(2)}, u32[]{:S(2)}) collective-permute-start(bf16[128,1536]{1,0:T(8,128)(2,1)S(1)} %fusion.51), channel_id=1, source_target_pairs={{0,4},{4,0},{1,5},{5,1},{2,6},{6,2},{3,7},{7,3},{8,12},{12,8},{9,1... | collective-permute-start | bytes 1179656 | tf_op jit(solution)/shard_map/ppermute | solution.py:27

commit v3 on v2

--- a/solution.py
+++ b/solution.py
@@ -66,28 +66,28 @@
     gz = place([out_grad] + [send(out_grad, "zl", k) for k in (1, 2, 3)], zl, 4)
     own1, own3 = (send(saved_input, "y", k) for k in (1, 3))
 
-    gz = after(gz, own1, own3)
-    gx = place([gz] + [send(gz, "x", k) for k in (1, 2, 3)], x, 4)
-    swapped = send(after(saved_input, own1), "zh", 1)
-    own2 = send(after(saved_input, own1), "y", 2)
+    gx1, gx3 = (send(gz, "x", k) for k in (1, 3))
+    swapped = send(after(saved_input, gz), "zh", 1)
+    gx2 = send(after(gz, own1), "x", 2)
+    gx = place([gz, gx1, gx2, gx3], x, 4)
+    own2 = send(after(saved_input, own3), "y", 2)
 
-    gc = place([gx, send(after(gx, swapped, own2), "c", 1)], c, 2)
-    far1, far3 = (send(swapped, "y", k) for k in (1, 3))
+    gc = place([gx, send(after(gx, own1, own3), "c", 1)], c, 2)
+    far1, far3, far2 = (send(swapped, "y", k) for k in (1, 3, 2))
     grads = gc.transpose(2, 1, 0, 3, 4).reshape(8 * tok, width)
     sums = lax.dot_general(grads, weight, (((1,), (1,)), ((), ())), preferred_element_type=jnp.float32)
     sums = sums.astype(jnp.bfloat16).reshape(2, 4, tok, hidden)
     p_other = lax.dynamic_index_in_dim(sums, 1 - zh, 0, keepdims=False)
     p_mine = lax.dynamic_index_in_dim(sums, zh, 0, keepdims=False)
 
-    p_ready = after(p_other, far1, far3)
+    p_ready = after(p_other, far1, far3, own2)
     r_other = [send(for_y(p_ready, k), "y", k) for k in (1, 3, 2)]
-    far2 = send(after(swapped, far1), "y", 2)
 
-    p_ready = after(p_mine, far2, r_other[0])
+    p_ready = after(p_mine, far2)
     r_mine = [send(for_y(p_ready, k), "y", k) for k in (1, 3, 2)]
     s_other = send(add_up(p_other, r_other).astype(jnp.bfloat16), "zh", 1)
 
-    own = [after(b, gz) for b in (saved_input, own1, own2, own3)]
+    own = [saved_input, own1, own2, own3]
     far = [after(b, sums) for b in (swapped, far1, far2, far3)]
     low = lax.dynamic_update_index_in_dim(jnp.zeros((2, 4 * tok, hidden), jnp.bfloat16), act(own), zh, 0)
     activated = lax.dynamic_update_index_in_dim(low, act(far), 1 - zh, 0).reshape(8 * tok, hidden)

time: 111 us -> 99.3 us (0.89)
  the two profiles are of different devices: /device:TPU:64 before, /device:TPU:32 now
where the time goes in v3:
time: 99.3 us; the launch traced here: 99 us
  starting transfers between devices  49.3 us (50%)
  waiting for transfers between devices  30.2 us (30%)
  matrix products  12.1 us (12%)
  other arithmetic  4.01 us (4%)
  local copies, waits for them, and re-layouts  2.26 us (2%)
  between operations  1.08 us (1%)
    ppermute x21, starting transfers between devices, send(): return lax.ppermute(v, axis, [(i, (i + step) % n) for i in range(n)])  49.3 us
    ppermute x21, waiting for transfers between devices, send(): return lax.ppermute(v, axis, [(i, (i + step) % n) for i in range(n)])  30.2 us
    dot_general x1, matrix products, body(): lax.dot_general(activated, grads, (((0,), (0,)), ((), ())), preferred_ele...  6.78 us
    dot_general x1, matrix products, body(): lax.dot_general(grads, weight, (((1,), (1,)), ((), ())), preferred_elemen...  5.3 us
    dynamic_update_slice x8, other arithmetic, act(): out = lax.dynamic_update_index_in_dim(out, a, lax.rem(y + (4 - k), 4), 0)  2.28 us
  transfers between devices with their start and end apart: 21, of which 7 were waited for; matrix products, arithmetic and copies ran while one was open for 17% of the time, Pallas kernels for 0%

profile of v3, /device:TPU:32, one launch (start us, length us, event | category | flops | bytes accessed | tf_op | source)
XLA Modules:
  0.0 99.0 jit_solution(10649277436185830732)
XLA Ops:
  0.6 2.0 %collective-permute-start.3 = (bf16[32,1536]{1,0:T(8,128)(2,1)}, bf16[32,1536]{1,0:T(8,128)(2,1)S(1)}, u32[]{:S(2)}, u32[]{:S(2)}) collective-permute-start(bf16[32,1536]{1,0:T(8,128)(2,1)} %param.3), channel_id=1, source_target_pairs={{0,64},{64,128},{128,192},{192,0},{1,65},{65,129},{129,193},{193,1... | collective-permute-start | bytes 294920 | tf_op jit(solution)/shard_map/ppermute | solution.py:27
  2.6 2.3 %collective-permute-start.4 = (bf16[32,1536]{1,0:T(8,128)(2,1)}, bf16[32,1536]{1,0:T(8,128)(2,1)S(1)}, u32[]{:S(2)}, u32[]{:S(2)}) collective-permute-start(bf16[32,1536]{1,0:T(8,128)(2,1)} %param.3), channel_id=1, source_target_pairs={{0,128},{64,192},{128,0},{192,64},{1,129},{65,193},{129,1},{193,65... | collective-permute-start | bytes 294920 | tf_op jit(solution)/shard_map/ppermute | solution.py:27
  4.9 1.1 %collective-permute-start.5 = (bf16[32,1536]{1,0:T(8,128)(2,1)}, bf16[32,1536]{1,0:T(8,128)(2,1)S(1)}, u32[]{:S(2)}, u32[]{:S(2)}) collective-permute-start(bf16[32,1536]{1,0:T(8,128)(2,1)} %param.3), channel_id=1, source_target_pairs={{0,192},{64,0},{128,64},{192,128},{1,193},{65,1},{129,65},{193,129... | collective-permute-start | bytes 294920 | tf_op jit(solution)/shard_map/ppermute | solution.py:27
  6.0 1.6 %collective-permute-start = (bf16[128,1536]{1,0:T(8,128)(2,1)}, bf16[128,1536]{1,0:T(8,128)(2,1)S(1)}, u32[]{:S(2)}, u32[]{:S(2)}) collective-permute-start(bf16[128,1536]{1,0:T(8,128)(2,1)} %param.4), channel_id=1, source_target_pairs={{0,1},{1,2},{2,3},{3,0},{4,5},{5,6},{6,7},{7,4},{8,9},{9,10},{10,1... | collective-permute-start | bytes 1179656 | tf_op jit(solution)/shard_map/ppermute | solution.py:27
  7.6 1.7 %collective-permute-start.1 = (bf16[128,1536]{1,0:T(8,128)(2,1)}, bf16[128,1536]{1,0:T(8,128)(2,1)S(1)}, u32[]{:S(2)}, u32[]{:S(2)}) collective-permute-start(bf16[128,1536]{1,0:T(8,128)(2,1)} %param.4), channel_id=1, source_target_pairs={{0,3},{1,0},{2,1},{3,2},{4,7},{5,4},{6,5},{7,6},{8,11},{9,8},{10,9... | collective-permute-start | bytes 1179656 | tf_op jit(solution)/shard_map/ppermute | solution.py:27
  9.4 0.3 fusion.67
  9.9 1.5 %collective-permute-done.4 = bf16[32,1536]{1,0:T(8,128)(2,1)S(1)} collective-permute-done((bf16[32,1536]{1,0:T(8,128)(2,1)}, bf16[32,1536]{1,0:T(8,128)(2,1)S(1)}, u32[]{:S(2)}, u32[]{:S(2)}) %collective-permute-start.4) | collective-permute-done | bytes 98336 | tf_op jit(solution)/shard_map/ppermute | solution.py:27
  11.4 2.0 %collective-permute-done.5 = bf16[32,1536]{1,0:T(8,128)(2,1)S(1)} collective-permute-done((bf16[32,1536]{1,0:T(8,128)(2,1)}, bf16[32,1536]{1,0:T(8,128)(2,1)S(1)}, u32[]{:S(2)}, u32[]{:S(2)}) %collective-permute-start.5) | collective-permute-done | bytes 98336 | tf_op jit(solution)/shard_map/ppermute | solution.py:27
  13.4 1.5 %collective-permute-start.7 = (bf16[4,32,1536]{2,1,0:T(8,128)(2,1)S(1)}, bf16[4,32,1536]{2,1,0:T(8,128)(2,1)S(1)}, u32[]{:S(2)}, u32[]{:S(2)}) collective-permute-start(bf16[4,32,1536]{2,1,0:T(8,128)(2,1)S(1)} %bitcast_dynamic-update-slice_fusion.8), channel_id=1, source_target_pairs={{0,16},{16,32},{32,48},{48,0},{1,17},{17,33},{33,49},{49,1},{2,18}... | collective-permute-start | bytes 1179656 | tf_op jit(solution)/shard_map/ppermute | solution.py:27
  14.9 1.8 %collective-permute-start.9 = (bf16[4,32,1536]{2,1,0:T(8,128)(2,1)S(1)}, bf16[4,32,1536]{2,1,0:T(8,128)(2,1)S(1)}, u32[]{:S(2)}, u32[]{:S(2)}) collective-permute-start(bf16[4,32,1536]{2,1,0:T(8,128)(2,1)S(1)} %bitcast_dynamic-update-slice_fusion.8), channel_id=1, source_target_pairs={{0,48},{16,0},{32,16},{48,32},{1,49},{17,1},{33,17},{49,33},{2,50}... | collective-permute-start | bytes 1179656 | tf_op jit(solution)/shard_map/ppermute | solution.py:27
  16.7 5.9 %collective-permute-start.6 = (bf16[128,1536]{1,0:T(8,128)(2,1)S(1)}, bf16[128,1536]{1,0:T(8,128)(2,1)S(1)}, u32[]{:S(2)}, u32[]{:S(2)}) collective-permute-start(bf16[128,1536]{1,0:T(8,128)(2,1)S(1)} %copy-done), channel_id=1, source_target_pairs={{0,4},{4,0},{1,5},{5,1},{2,6},{6,2},{3,7},{7,3},{8,12},{12,8},{9,1... | collective-permute-start | bytes 1179656 | tf_op jit(solution)/shard_map/ppermute | solution.py:27
  22.8 1.9 %collective-permute-start.8 = (bf16[4,32,1536]{2,1,0:T(8,128)(2,1)S(1)}, bf16[4,32,1536]{2,1,0:T(8,128)(2,1)S(1)}, u32[]{:S(2)}, u32[]{:S(2)}) collective-permute-start(bf16[4,32,1536]{2,1,0:T(8,128)(2,1)S(1)} %bitcast_dynamic-update-slice_fusion.8), channel_id=1, source_target_pairs={{0,32},{16,48},{32,0},{48,16},{1,33},{17,49},{33,1},{49,17},{2,34}... | collective-permute-start | bytes 1179656 | tf_op jit(solution)/shard_map/ppermute | solution.py:27
  24.7 3.2 %collective-permute-start.2 = (bf16[128,1536]{1,0:T(8,128)(2,1)S(1)}, bf16[128,1536]{1,0:T(8,128)(2,1)S(1)}, u32[]{:S(2)}, u32[]{:S(2)}) collective-permute-start(bf16[128,1536]{1,0:T(8,128)(2,1)S(1)} %copy-done), channel_id=1, source_target_pairs={{0,2},{1,3},{2,0},{3,1},{4,6},{5,7},{6,4},{7,5},{8,10},{9,11},{10,... | collective-permute-start | bytes 1179656 | tf_op jit(solution)/shard_map/ppermute | solution.py:27
  28.2 11.6 %collective-permute-done.6 = bf16[128,1536]{1,0:T(8,128)(2,1)S(1)} collective-permute-done((bf16[128,1536]{1,0:T(8,128)(2,1)S(1)}, bf16[128,1536]{1,0:T(8,128)(2,1)S(1)}, u32[]{:S(2)}, u32[]{:S(2)}) %collective-permute-start.6) | collective-permute-done | bytes 393248 | tf_op jit(solution)/shard_map/ppermute | solution.py:27
  39.7 1.6 %collective-permute-start.11 = (bf16[128,1536]{1,0:T(8,128)(2,1)S(1)}, bf16[128,1536]{1,0:T(8,128)(2,1)S(1)}, u32[]{:S(2)}, u32[]{:S(2)}) collective-permute-start(bf16[128,1536]{1,0:T(8,128)(2,1)S(1)} %collective-permute-done.6), channel_id=1, source_target_pairs={{0,1},{1,2},{2,3},{3,0},{4,5},{5,6},{6,7},{7,4},{8,9},{9,10},{10,1... | collective-permute-start | bytes 1179656 | tf_op jit(solution)/shard_map/ppermute | solution.py:27
  41.3 1.7 %collective-permute-start.13 = (bf16[128,1536]{1,0:T(8,128)(2,1)S(1)}, bf16[128,1536]{1,0:T(8,128)(2,1)S(1)}, u32[]{:S(2)}, u32[]{:S(2)}) collective-permute-start(bf16[128,1536]{1,0:T(8,128)(2,1)S(1)} %collective-permute-done.6), channel_id=1, source_target_pairs={{0,3},{1,0},{2,1},{3,2},{4,7},{5,4},{6,5},{7,6},{8,11},{9,8},{10,9... | collective-permute-start | bytes 1179656 | tf_op jit(solution)/shard_map/ppermute | solution.py:27
  43.0 2.1 %collective-permute-start.12 = (bf16[128,1536]{1,0:T(8,128)(2,1)S(1)}, bf16[128,1536]{1,0:T(8,128)(2,1)S(1)}, u32[]{:S(2)}, u32[]{:S(2)}) collective-permute-start(bf16[128,1536]{1,0:T(8,128)(2,1)S(1)} %collective-permute-done.6), channel_id=1, source_target_pairs={{0,2},{1,3},{2,0},{3,1},{4,6},{5,7},{6,4},{7,5},{8,10},{9,11},{10,... | collective-permute-start | bytes 1179656 | tf_op jit(solution)/shard_map/ppermute | solution.py:27
  46.5 0.3 broadcast_in_dim.88
  47.0 1.8 %collective-permute-done.10 = bf16[4,4,32,1536]{3,2,0,1:T(8,128)(2,1)S(1)} collective-permute-done((bf16[4,4,32,1536]{3,2,0,1:T(8,128)(2,1)S(1)}, bf16[4,4,32,1536]{3,2,0,1:T(8,128)(2,1)S(1)}, u32[]{:S(2)}, u32[]{:S(2)}) %collective-permute-start.10) | collective-permute-done | bytes 1572896 | tf_op jit(solution)/shard_map/ppermute | solution.py:27
  49.1 5.3 %convolution_convert_fusion.1 = bf16[1024,1536]{1,0:T(8,128)(2,1)S(1)} fusion(bf16[1024,1536]{1,0:T(8,128)(2,1)S(1)} %bitcast.103, bf16[1536,1536]{1,0:T(8,128)(2,1)S(1)} %bitcast.106), kind=kOutput, calls=%fused_computation.1 | convolution fusion | flops 4833411072 | bytes 11010048 | tf_op jit(solution)/shard_map/dot_general | solution.py:78
  54.7 0.8 collective-permute-start.17
  55.5 6.6 %collective-permute-start.18 = (bf16[128,1536]{1,0:T(8,128)(2,1)S(1)}, bf16[128,1536]{1,0:T(8,128)(2,1)S(1)}, u32[]{:S(2)}, u32[]{:S(2)}) collective-permute-start(bf16[128,1536]{1,0:T(8,128)(2,1)S(1)} %get-tuple-element.29), channel_id=1, source_target_pairs={{0,3},{1,0},{2,1},{3,2},{4,7},{5,4},{6,5},{7,6},{8,11},{9,8},{10,9... | collective-permute-start | bytes 1179656 | tf_op jit(solution)/shard_map/ppermute | solution.py:27
  62.1 1.4 %collective-permute-start.19 = (bf16[128,1536]{1,0:T(8,128)(2,1)S(1)}, bf16[128,1536]{1,0:T(8,128)(2,1)S(1)}, u32[]{:S(2)}, u32[]{:S(2)}) collective-permute-start(bf16[128,1536]{1,0:T(8,128)(2,1)S(1)} %get-tuple-element.28), channel_id=1, source_target_pairs={{0,2},{1,3},{2,0},{3,1},{4,6},{5,7},{6,4},{7,5},{8,10},{9,11},{10,... | collective-permute-start | bytes 1179656 | tf_op jit(solution)/shard_map/ppermute | solution.py:27
  63.5 1.5 %collective-permute-start.14 = (bf16[128,1536]{1,0:T(8,128)(2,1)S(1)}, bf16[128,1536]{1,0:T(8,128)(2,1)S(1)}, u32[]{:S(2)}, u32[]{:S(2)}) collective-permute-start(bf16[128,1536]{1,0:T(8,128)(2,1)S(1)} %get-tuple-element.24), channel_id=1, source_target_pairs={{0,1},{1,2},{2,3},{3,0},{4,5},{5,6},{6,7},{7,4},{8,9},{9,10},{10,1... | collective-permute-start | bytes 1179656 | tf_op jit(solution)/shard_map/ppermute | solution.py:27
  65.0 1.8 %collective-permute-start.15 = (bf16[128,1536]{1,0:T(8,128)(2,1)S(1)}, bf16[128,1536]{1,0:T(8,128)(2,1)S(1)}, u32[]{:S(2)}, u32[]{:S(2)}) collective-permute-start(bf16[128,1536]{1,0:T(8,128)(2,1)S(1)} %get-tuple-element.26), channel_id=1, source_target_pairs={{0,3},{1,0},{2,1},{3,2},{4,7},{5,4},{6,5},{7,6},{8,11},{9,8},{10,9... | collective-permute-start | bytes 1179656 | tf_op jit(solution)/shard_map/ppermute | solution.py:27
  68.3 10.6 %collective-permute-done.17 = bf16[128,1536]{1,0:T(8,128)(2,1)S(1)} collective-permute-done((bf16[128,1536]{1,0:T(8,128)(2,1)S(1)}, bf16[128,1536]{1,0:T(8,128)(2,1)S(1)}, u32[]{:S(2)}, u32[]{:S(2)}) %collective-permute-start.17) | collective-permute-done | bytes 393248 | tf_op jit(solution)/shard_map/ppermute | solution.py:27
  78.9 2.6 %collective-permute-start.16 = (bf16[128,1536]{1,0:T(8,128)(2,1)S(1)}, bf16[128,1536]{1,0:T(8,128)(2,1)S(1)}, u32[]{:S(2)}, u32[]{:S(2)}) collective-permute-start(bf16[128,1536]{1,0:T(8,128)(2,1)S(1)} %get-tuple-element.25), channel_id=1, source_target_pairs={{0,2},{1,3},{2,0},{3,1},{4,6},{5,7},{6,4},{7,5},{8,10},{9,11},{10,... | collective-permute-start | bytes 1179656 | tf_op jit(solution)/shard_map/ppermute | solution.py:27
  81.6 0.3 collective-permute-done.19
  82.2 6.2 %collective-permute-start.20 = (bf16[128,1536]{1,0:T(8,128)(2,1)S(1)}, bf16[128,1536]{1,0:T(8,128)(2,1)S(1)}, u32[]{:S(2)}, u32[]{:S(2)}) collective-permute-start(bf16[128,1536]{1,0:T(8,128)(2,1)S(1)} %fusion.48), channel_id=1, source_target_pairs={{0,4},{4,0},{1,5},{5,1},{2,6},{6,2},{3,7},{7,3},{8,12},{12,8},{9,1... | collective-permute-start | bytes 1179656 | tf_op jit(solution)/shard_map/ppermute | solution.py:27
  88.4 6.8 %convolution_convert_fusion = bf16[1536,1536]{1,0:T(8,128)(2,1)} fusion(bf16[1024,1536]{1,0:T(8,128)(2,1)S(1)} %bitcast.102, bf16[1024,1536]{1,0:T(8,128)(2,1)S(1)} %bitcast.104), kind=kOutput, calls=%fused_computation | convolution fusion | flops 4834197504 | bytes 11010048 | tf_op jit(solution)/shard_map/dot_general | solution.py:94
  95.1 2.4 %collective-permute-done.20 = bf16[128,1536]{1,0:T(8,128)(2,1)S(1)} collective-permute-done((bf16[128,1536]{1,0:T(8,128)(2,1)S(1)}, bf16[128,1536]{1,0:T(8,128)(2,1)S(1)}, u32[]{:S(2)}, u32[]{:S(2)}) %collective-permute-start.20) | collective-permute-done | bytes 393248 | tf_op jit(solution)/shard_map/ppermute | solution.py:27
  97.5 1.5 %fusion.7 = bf16[128,1536]{1,0:T(8,128)(2,1)} fusion(bf16[128,1536]{1,0:T(8,128)(2,1)S(1)} %copy-done, bf16[128,1536]{1,0:T(8,128)(2,1)S(1)} %collective-permute-done.20, bf16[128,1536]{1,0:T(8,128)(2,1)S(1)} %collective-permute-done.16, bf16[128,1536]{1,0:T(8,128)(2,1)S(1)} %collective-permute-done.15, bf16[128,1536]{1,0:T(8,128)(2,1)S(1)} %collective-permute-done.14, ...), kind=kLoop, calls=%fused_computation.57 | loop fusion | flops 5701632 | bytes 2752520 | tf_op jit(solution)/shard_map/convert_element_type | solution.py:98
  (52 shorter events, 4.4 us)
Async XLA Ops:
  0.6 9.1 %copy-start.1 = (bf16[32,1536]{1,0:T(8,128)(2,1)S(1)}, bf16[32,1536]{1,0:T(8,128)(2,1)}, u32[]{:S(2)}) copy-start(bf16[32,1536]{1,0:T(8,128)(2,1)} %param.3) | copy-start | bytes 294916
  0.6 8.7 %copy-start = (bf16[128,1536]{1,0:T(8,128)(2,1)S(1)}, bf16[128,1536]{1,0:T(8,128)(2,1)}, u32[]{:S(2)}) copy-start(bf16[128,1536]{1,0:T(8,128)(2,1)} %param.4) | copy-start | bytes 1179652
  0.6 9.2 %collective-permute-start.3 = (bf16[32,1536]{1,0:T(8,128)(2,1)}, bf16[32,1536]{1,0:T(8,128)(2,1)S(1)}, u32[]{:S(2)}, u32[]{:S(2)}) collective-permute-start(bf16[32,1536]{1,0:T(8,128)(2,1)} %param.3), channel_id=1, source_target_pairs={{0,64},{64,128},{128,192},{192,0},{1,65},{65,129},{129,193},{193,1... | collective-permute-start | bytes 294920 | tf_op jit(solution)/shard_map/ppermute | solution.py:27
  2.6 8.8 %collective-permute-start.4 = (bf16[32,1536]{1,0:T(8,128)(2,1)}, bf16[32,1536]{1,0:T(8,128)(2,1)S(1)}, u32[]{:S(2)}, u32[]{:S(2)}) collective-permute-start(bf16[32,1536]{1,0:T(8,128)(2,1)} %param.3), channel_id=1, source_target_pairs={{0,128},{64,192},{128,0},{192,64},{1,129},{65,193},{129,1},{193,65... | collective-permute-start | bytes 294920 | tf_op jit(solution)/shard_map/ppermute | solution.py:27
  4.9 8.5 %collective-permute-start.5 = (bf16[32,1536]{1,0:T(8,128)(2,1)}, bf16[32,1536]{1,0:T(8,128)(2,1)S(1)}, u32[]{:S(2)}, u32[]{:S(2)}) collective-permute-start(bf16[32,1536]{1,0:T(8,128)(2,1)} %param.3), channel_id=1, source_target_pairs={{0,192},{64,0},{128,64},{192,128},{1,193},{65,1},{129,65},{193,129... | collective-permute-start | bytes 294920 | tf_op jit(solution)/shard_map/ppermute | solution.py:27
  6.0 16.8 %collective-permute-start = (bf16[128,1536]{1,0:T(8,128)(2,1)}, bf16[128,1536]{1,0:T(8,128)(2,1)S(1)}, u32[]{:S(2)}, u32[]{:S(2)}) collective-permute-start(bf16[128,1536]{1,0:T(8,128)(2,1)} %param.4), channel_id=1, source_target_pairs={{0,1},{1,2},{2,3},{3,0},{4,5},{5,6},{6,7},{7,4},{8,9},{9,10},{10,1... | collective-permute-start | bytes 1179656 | tf_op jit(solution)/shard_map/ppermute | solution.py:27
  7.6 17.1 %collective-permute-start.1 = (bf16[128,1536]{1,0:T(8,128)(2,1)}, bf16[128,1536]{1,0:T(8,128)(2,1)S(1)}, u32[]{:S(2)}, u32[]{:S(2)}) collective-permute-start(bf16[128,1536]{1,0:T(8,128)(2,1)} %param.4), channel_id=1, source_target_pairs={{0,3},{1,0},{2,1},{3,2},{4,7},{5,4},{6,5},{7,6},{8,11},{9,8},{10,9... | collective-permute-start | bytes 1179656 | tf_op jit(solution)/shard_map/ppermute | solution.py:27
  13.4 27.9 %collective-permute-start.7 = (bf16[4,32,1536]{2,1,0:T(8,128)(2,1)S(1)}, bf16[4,32,1536]{2,1,0:T(8,128)(2,1)S(1)}, u32[]{:S(2)}, u32[]{:S(2)}) collective-permute-start(bf16[4,32,1536]{2,1,0:T(8,128)(2,1)S(1)} %bitcast_dynamic-update-slice_fusion.8), channel_id=1, source_target_pairs={{0,16},{16,32},{32,48},{48,0},{1,17},{17,33},{33,49},{49,1},{2,18}... | collective-permute-start | bytes 1179656 | tf_op jit(solution)/shard_map/ppermute | solution.py:27
  14.9 30.2 %collective-permute-start.9 = (bf16[4,32,1536]{2,1,0:T(8,128)(2,1)S(1)}, bf16[4,32,1536]{2,1,0:T(8,128)(2,1)S(1)}, u32[]{:S(2)}, u32[]{:S(2)}) collective-permute-start(bf16[4,32,1536]{2,1,0:T(8,128)(2,1)S(1)} %bitcast_dynamic-update-slice_fusion.8), channel_id=1, source_target_pairs={{0,48},{16,0},{32,16},{48,32},{1,49},{17,1},{33,17},{49,33},{2,50}... | collective-permute-start | bytes 1179656 | tf_op jit(solution)/shard_map/ppermute | solution.py:27
  16.7 23.0 %collective-permute-start.6 = (bf16[128,1536]{1,0:T(8,128)(2,1)S(1)}, bf16[128,1536]{1,0:T(8,128)(2,1)S(1)}, u32[]{:S(2)}, u32[]{:S(2)}) collective-permute-start(bf16[128,1536]{1,0:T(8,128)(2,1)S(1)} %copy-done), channel_id=1, source_target_pairs={{0,4},{4,0},{1,5},{5,1},{2,6},{6,2},{3,7},{7,3},{8,12},{12,8},{9,1... | collective-permute-start | bytes 1179656 | tf_op jit(solution)/shard_map/ppermute | solution.py:27
  22.8 20.2 %collective-permute-start.8 = (bf16[4,32,1536]{2,1,0:T(8,128)(2,1)S(1)}, bf16[4,32,1536]{2,1,0:T(8,128)(2,1)S(1)}, u32[]{:S(2)}, u32[]{:S(2)}) collective-permute-start(bf16[4,32,1536]{2,1,0:T(8,128)(2,1)S(1)} %bitcast_dynamic-update-slice_fusion.8), channel_id=1, source_target_pairs={{0,32},{16,48},{32,0},{48,16},{1,33},{17,49},{33,1},{49,17},{2,34}... | collective-permute-start | bytes 1179656 | tf_op jit(solution)/shard_map/ppermute | solution.py:27
  24.7 20.8 %collective-permute-start.2 = (bf16[128,1536]{1,0:T(8,128)(2,1)S(1)}, bf16[128,1536]{1,0:T(8,128)(2,1)S(1)}, u32[]{:S(2)}, u32[]{:S(2)}) collective-permute-start(bf16[128,1536]{1,0:T(8,128)(2,1)S(1)} %copy-done), channel_id=1, source_target_pairs={{0,2},{1,3},{2,0},{3,1},{4,6},{5,7},{6,4},{7,5},{8,10},{9,11},{10,... | collective-permute-start | bytes 1179656 | tf_op jit(solution)/shard_map/ppermute | solution.py:27
  39.7 14.9 %collective-permute-start.11 = (bf16[128,1536]{1,0:T(8,128)(2,1)S(1)}, bf16[128,1536]{1,0:T(8,128)(2,1)S(1)}, u32[]{:S(2)}, u32[]{:S(2)}) collective-permute-start(bf16[128,1536]{1,0:T(8,128)(2,1)S(1)} %collective-permute-done.6), channel_id=1, source_target_pairs={{0,1},{1,2},{2,3},{3,0},{4,5},{5,6},{6,7},{7,4},{8,9},{9,10},{10,1... | collective-permute-start | bytes 1179656 | tf_op jit(solution)/shard_map/ppermute | solution.py:27
  41.3 13.3 %collective-permute-start.13 = (bf16[128,1536]{1,0:T(8,128)(2,1)S(1)}, bf16[128,1536]{1,0:T(8,128)(2,1)S(1)}, u32[]{:S(2)}, u32[]{:S(2)}) collective-permute-start(bf16[128,1536]{1,0:T(8,128)(2,1)S(1)} %collective-permute-done.6), channel_id=1, source_target_pairs={{0,3},{1,0},{2,1},{3,2},{4,7},{5,4},{6,5},{7,6},{8,11},{9,8},{10,9... | collective-permute-start | bytes 1179656 | tf_op jit(solution)/shard_map/ppermute | solution.py:27
  43.0 20.4 %collective-permute-start.12 = (bf16[128,1536]{1,0:T(8,128)(2,1)S(1)}, bf16[128,1536]{1,0:T(8,128)(2,1)S(1)}, u32[]{:S(2)}, u32[]{:S(2)}) collective-permute-start(bf16[128,1536]{1,0:T(8,128)(2,1)S(1)} %collective-permute-done.6), channel_id=1, source_target_pairs={{0,2},{1,3},{2,0},{3,1},{4,6},{5,7},{6,4},{7,5},{8,10},{9,11},{10,... | collective-permute-start | bytes 1179656 | tf_op jit(solution)/shard_map/ppermute | solution.py:27
  45.2 3.7 %collective-permute-start.10 = (bf16[4,4,32,1536]{3,2,0,1:T(8,128)(2,1)S(1)}, bf16[4,4,32,1536]{3,2,0,1:T(8,128)(2,1)S(1)}, u32[]{:S(2)}, u32[]{:S(2)}) collective-permute-start(bf16[4,4,32,1536]{3,2,0,1:T(8,128)(2,1)S(1)} %bitcast_dynamic-update-slice_fusion.7), channel_id=1, source_target_pairs={{0,8},{8,0},{1,9},{9,1},{2,10},{10,2},{3,11},{11,3},{4,12},{12,4},... | collective-permute-start | bytes 4718600 | tf_op jit(solution)/shard_map/ppermute | solution.py:27
  46.1 3.0 %slice-start = ((s8[4718592]{0:T(1024)(128)(4,1)}), s8[4194304]{0:T(1024)(128)(4,1)S(1)}, s32[]{:S(2)}) async-start(s8[4718592]{0:T(1024)(128)(4,1)} %bitcast.105), calls=%async_computation | async-start | bytes 8388608
  46.4 2.6 %slice-start.1 = ((s8[4718592]{0:T(1024)(128)(4,1)}), s8[524288]{0:T(1024)(128)(4,1)S(1)}, s32[]{:S(2)}) async-start(s8[4718592]{0:T(1024)(128)(4,1)} %bitcast.105), calls=%async_computation.1 | async-start | bytes 1048576
  54.7 24.2 %collective-permute-start.17 = (bf16[128,1536]{1,0:T(8,128)(2,1)S(1)}, bf16[128,1536]{1,0:T(8,128)(2,1)S(1)}, u32[]{:S(2)}, u32[]{:S(2)}) collective-permute-start(bf16[128,1536]{1,0:T(8,128)(2,1)S(1)} %get-tuple-element.27), channel_id=1, source_target_pairs={{0,1},{1,2},{2,3},{3,0},{4,5},{5,6},{6,7},{7,4},{8,9},{9,10},{10,1... | collective-permute-start | bytes 1179656 | tf_op jit(solution)/shard_map/ppermute | solution.py:27
  55.5 26.1 %collective-permute-start.18 = (bf16[128,1536]{1,0:T(8,128)(2,1)S(1)}, bf16[128,1536]{1,0:T(8,128)(2,1)S(1)}, u32[]{:S(2)}, u32[]{:S(2)}) collective-permute-start(bf16[128,1536]{1,0:T(8,128)(2,1)S(1)} %get-tuple-element.29), channel_id=1, source_target_pairs={{0,3},{1,0},{2,1},{3,2},{4,7},{5,4},{6,5},{7,6},{8,11},{9,8},{10,9... | collective-permute-start | bytes 1179656 | tf_op jit(solution)/shard_map/ppermute | solution.py:27
  62.1 19.9 %collective-permute-start.19 = (bf16[128,1536]{1,0:T(8,128)(2,1)S(1)}, bf16[128,1536]{1,0:T(8,128)(2,1)S(1)}, u32[]{:S(2)}, u32[]{:S(2)}) collective-permute-start(bf16[128,1536]{1,0:T(8,128)(2,1)S(1)} %get-tuple-element.28), channel_id=1, source_target_pairs={{0,2},{1,3},{2,0},{3,1},{4,6},{5,7},{6,4},{7,5},{8,10},{9,11},{10,... | collective-permute-start | bytes 1179656 | tf_op jit(solution)/shard_map/ppermute | solution.py:27
  63.5 31.6 %collective-permute-start.14 = (bf16[128,1536]{1,0:T(8,128)(2,1)S(1)}, bf16[128,1536]{1,0:T(8,128)(2,1)S(1)}, u32[]{:S(2)}, u32[]{:S(2)}) collective-permute-start(bf16[128,1536]{1,0:T(8,128)(2,1)S(1)} %get-tuple-element.24), channel_id=1, source_target_pairs={{0,1},{1,2},{2,3},{3,0},{4,5},{5,6},{6,7},{7,4},{8,9},{9,10},{10,1... | collective-permute-start | bytes 1179656 | tf_op jit(solution)/shard_map/ppermute | solution.py:27
  65.0 30.1 %collective-permute-start.15 = (bf16[128,1536]{1,0:T(8,128)(2,1)S(1)}, bf16[128,1536]{1,0:T(8,128)(2,1)S(1)}, u32[]{:S(2)}, u32[]{:S(2)}) collective-permute-start(bf16[128,1536]{1,0:T(8,128)(2,1)S(1)} %get-tuple-element.26), channel_id=1, source_target_pairs={{0,3},{1,0},{2,1},{3,2},{4,7},{5,4},{6,5},{7,6},{8,11},{9,8},{10,9... | collective-permute-start | bytes 1179656 | tf_op jit(solution)/shard_map/ppermute | solution.py:27
  78.9 16.2 %collective-permute-start.16 = (bf16[128,1536]{1,0:T(8,128)(2,1)S(1)}, bf16[128,1536]{1,0:T(8,128)(2,1)S(1)}, u32[]{:S(2)}, u32[]{:S(2)}) collective-permute-start(bf16[128,1536]{1,0:T(8,128)(2,1)S(1)} %get-tuple-element.25), channel_id=1, source_target_pairs={{0,2},{1,3},{2,0},{3,1},{4,6},{5,7},{6,4},{7,5},{8,10},{9,11},{10,... | collective-permute-start | bytes 1179656 | tf_op jit(solution)/shard_map/ppermute | solution.py:27
  82.2 15.3 %collective-permute-start.20 = (bf16[128,1536]{1,0:T(8,128)(2,1)S(1)}, bf16[128,1536]{1,0:T(8,128)(2,1)S(1)}, u32[]{:S(2)}, u32[]{:S(2)}) collective-permute-start(bf16[128,1536]{1,0:T(8,128)(2,1)S(1)} %fusion.48), channel_id=1, source_target_pairs={{0,4},{4,0},{1,5},{5,1},{2,6},{6,2},{3,7},{7,3},{8,12},{12,8},{9,1... | collective-permute-start | bytes 1179656 | tf_op jit(solution)/shard_map/ppermute | solution.py:27

commit v4 on v3

--- a/solution.py
+++ b/solution.py
@@ -73,17 +73,19 @@
     own2 = send(after(saved_input, own3), "y", 2)
 
     gc = place([gx, send(after(gx, own1, own3), "c", 1)], c, 2)
-    far1, far3, far2 = (send(swapped, "y", k) for k in (1, 3, 2))
+    turn = after(swapped, gc)
+    far1, far3 = (send(turn, "y", k) for k in (1, 3))
+    far2 = send(after(own2, gc, swapped), "zh", 1)
     grads = gc.transpose(2, 1, 0, 3, 4).reshape(8 * tok, width)
     sums = lax.dot_general(grads, weight, (((1,), (1,)), ((), ())), preferred_element_type=jnp.float32)
     sums = sums.astype(jnp.bfloat16).reshape(2, 4, tok, hidden)
     p_other = lax.dynamic_index_in_dim(sums, 1 - zh, 0, keepdims=False)
     p_mine = lax.dynamic_index_in_dim(sums, zh, 0, keepdims=False)
 
-    p_ready = after(p_other, far1, far3, own2)
+    p_ready = p_other
     r_other = [send(for_y(p_ready, k), "y", k) for k in (1, 3, 2)]
 
-    p_ready = after(p_mine, far2)
+    p_ready = after(p_mine, far1, far3, far2, r_other[0])
     r_mine = [send(for_y(p_ready, k), "y", k) for k in (1, 3, 2)]
     s_other = send(add_up(p_other, r_other).astype(jnp.bfloat16), "zh", 1)
 

time: 99.3 us -> 96.4 us (0.971)
  starting transfers between devices: 49.3 us -> 47.1 us
    ppermute x21, starting transfers between devices: 49.3 us -> 47.1 us  [send(): return lax.ppermute(v, axis, [(i, (i + step) % n) for i in range(n)])]
  transfers between devices with their start and end apart: 21 -> 21, of which waited for: 7 -> 11; matrix products, arithmetic and copies ran while one was open for 17% -> 17% of each run, Pallas kernels for 0% -> 0%
where the time goes in v4:
time: 96.4 us; the launch traced here: 96.3 us
  starting transfers between devices  47.1 us (49%)
  waiting for transfers between devices  29.9 us (31%)
  matrix products  12.1 us (13%)
  other arithmetic  4 us (4%)
  local copies, waits for them, and re-layouts  2.15 us (2%)
  between operations  1.03 us (1%)
    ppermute x21, starting transfers between devices, send(): return lax.ppermute(v, axis, [(i, (i + step) % n) for i in range(n)])  47.1 us
    ppermute x21, waiting for transfers between devices, send(): return lax.ppermute(v, axis, [(i, (i + step) % n) for i in range(n)])  29.9 us
    dot_general x1, matrix products, body(): lax.dot_general(activated, grads, (((0,), (0,)), ((), ())), preferred_ele...  6.8 us
    dot_general x1, matrix products, body(): lax.dot_general(grads, weight, (((1,), (1,)), ((), ())), preferred_elemen...  5.29 us
    dynamic_update_slice x8, other arithmetic, act(): out = lax.dynamic_update_index_in_dim(out, a, lax.rem(y + (4 - k), 4), 0)  2.27 us
  transfers between devices with their start and end apart: 21, of which 11 were waited for; matrix products, arithmetic and copies ran while one was open for 17% of the time, Pallas kernels for 0%

profile of v4, /device:TPU:32, one launch (start us, length us, event | category | flops | bytes accessed | tf_op | source)
XLA Modules:
  0.0 96.3 jit_solution(15850613319265449364)
XLA Ops:
  0.6 2.0 %collective-permute-start.3 = (bf16[32,1536]{1,0:T(8,128)(2,1)}, bf16[32,1536]{1,0:T(8,128)(2,1)S(1)}, u32[]{:S(2)}, u32[]{:S(2)}) collective-permute-start(bf16[32,1536]{1,0:T(8,128)(2,1)} %param.3), channel_id=1, source_target_pairs={{0,64},{64,128},{128,192},{192,0},{1,65},{65,129},{129,193},{193,1... | collective-permute-start | bytes 294920 | tf_op jit(solution)/shard_map/ppermute | solution.py:27
  2.6 2.3 %collective-permute-start.4 = (bf16[32,1536]{1,0:T(8,128)(2,1)}, bf16[32,1536]{1,0:T(8,128)(2,1)S(1)}, u32[]{:S(2)}, u32[]{:S(2)}) collective-permute-start(bf16[32,1536]{1,0:T(8,128)(2,1)} %param.3), channel_id=1, source_target_pairs={{0,128},{64,192},{128,0},{192,64},{1,129},{65,193},{129,1},{193,65... | collective-permute-start | bytes 294920 | tf_op jit(solution)/shard_map/ppermute | solution.py:27
  4.9 1.1 %collective-permute-start.5 = (bf16[32,1536]{1,0:T(8,128)(2,1)}, bf16[32,1536]{1,0:T(8,128)(2,1)S(1)}, u32[]{:S(2)}, u32[]{:S(2)}) collective-permute-start(bf16[32,1536]{1,0:T(8,128)(2,1)} %param.3), channel_id=1, source_target_pairs={{0,192},{64,0},{128,64},{192,128},{1,193},{65,1},{129,65},{193,129... | collective-permute-start | bytes 294920 | tf_op jit(solution)/shard_map/ppermute | solution.py:27
  6.0 1.6 %collective-permute-start = (bf16[128,1536]{1,0:T(8,128)(2,1)}, bf16[128,1536]{1,0:T(8,128)(2,1)S(1)}, u32[]{:S(2)}, u32[]{:S(2)}) collective-permute-start(bf16[128,1536]{1,0:T(8,128)(2,1)} %param.4), channel_id=1, source_target_pairs={{0,1},{1,2},{2,3},{3,0},{4,5},{5,6},{6,7},{7,4},{8,9},{9,10},{10,1... | collective-permute-start | bytes 1179656 | tf_op jit(solution)/shard_map/ppermute | solution.py:27
  7.6 1.7 %collective-permute-start.1 = (bf16[128,1536]{1,0:T(8,128)(2,1)}, bf16[128,1536]{1,0:T(8,128)(2,1)S(1)}, u32[]{:S(2)}, u32[]{:S(2)}) collective-permute-start(bf16[128,1536]{1,0:T(8,128)(2,1)} %param.4), channel_id=1, source_target_pairs={{0,3},{1,0},{2,1},{3,2},{4,7},{5,4},{6,5},{7,6},{8,11},{9,8},{10,9... | collective-permute-start | bytes 1179656 | tf_op jit(solution)/shard_map/ppermute | solution.py:27
  9.9 1.5 %collective-permute-done.4 = bf16[32,1536]{1,0:T(8,128)(2,1)S(1)} collective-permute-done((bf16[32,1536]{1,0:T(8,128)(2,1)}, bf16[32,1536]{1,0:T(8,128)(2,1)S(1)}, u32[]{:S(2)}, u32[]{:S(2)}) %collective-permute-start.4) | collective-permute-done | bytes 98336 | tf_op jit(solution)/shard_map/ppermute | solution.py:27
  11.4 2.0 %collective-permute-done.5 = bf16[32,1536]{1,0:T(8,128)(2,1)S(1)} collective-permute-done((bf16[32,1536]{1,0:T(8,128)(2,1)}, bf16[32,1536]{1,0:T(8,128)(2,1)S(1)}, u32[]{:S(2)}, u32[]{:S(2)}) %collective-permute-start.5) | collective-permute-done | bytes 98336 | tf_op jit(solution)/shard_map/ppermute | solution.py:27
  13.4 1.5 %collective-permute-start.7 = (bf16[4,32,1536]{2,1,0:T(8,128)(2,1)S(1)}, bf16[4,32,1536]{2,1,0:T(8,128)(2,1)S(1)}, u32[]{:S(2)}, u32[]{:S(2)}) collective-permute-start(bf16[4,32,1536]{2,1,0:T(8,128)(2,1)S(1)} %bitcast_dynamic-update-slice_fusion.8), channel_id=1, source_target_pairs={{0,16},{16,32},{32,48},{48,0},{1,17},{17,33},{33,49},{49,1},{2,18}... | collective-permute-start | bytes 1179656 | tf_op jit(solution)/shard_map/ppermute | solution.py:27
  14.9 1.8 %collective-permute-start.9 = (bf16[4,32,1536]{2,1,0:T(8,128)(2,1)S(1)}, bf16[4,32,1536]{2,1,0:T(8,128)(2,1)S(1)}, u32[]{:S(2)}, u32[]{:S(2)}) collective-permute-start(bf16[4,32,1536]{2,1,0:T(8,128)(2,1)S(1)} %bitcast_dynamic-update-slice_fusion.8), channel_id=1, source_target_pairs={{0,48},{16,0},{32,16},{48,32},{1,49},{17,1},{33,17},{49,33},{2,50}... | collective-permute-start | bytes 1179656 | tf_op jit(solution)/shard_map/ppermute | solution.py:27
  16.7 5.9 %collective-permute-start.6 = (bf16[128,1536]{1,0:T(8,128)(2,1)S(1)}, bf16[128,1536]{1,0:T(8,128)(2,1)S(1)}, u32[]{:S(2)}, u32[]{:S(2)}) collective-permute-start(bf16[128,1536]{1,0:T(8,128)(2,1)S(1)} %copy-done), channel_id=1, source_target_pairs={{0,4},{4,0},{1,5},{5,1},{2,6},{6,2},{3,7},{7,3},{8,12},{12,8},{9,1... | collective-permute-start | bytes 1179656 | tf_op jit(solution)/shard_map/ppermute | solution.py:27
  22.8 1.9 %collective-permute-start.8 = (bf16[4,32,1536]{2,1,0:T(8,128)(2,1)S(1)}, bf16[4,32,1536]{2,1,0:T(8,128)(2,1)S(1)}, u32[]{:S(2)}, u32[]{:S(2)}) collective-permute-start(bf16[4,32,1536]{2,1,0:T(8,128)(2,1)S(1)} %bitcast_dynamic-update-slice_fusion.8), channel_id=1, source_target_pairs={{0,32},{16,48},{32,0},{48,16},{1,33},{17,49},{33,1},{49,17},{2,34}... | collective-permute-start | bytes 1179656 | tf_op jit(solution)/shard_map/ppermute | solution.py:27
  24.7 3.2 %collective-permute-start.2 = (bf16[128,1536]{1,0:T(8,128)(2,1)S(1)}, bf16[128,1536]{1,0:T(8,128)(2,1)S(1)}, u32[]{:S(2)}, u32[]{:S(2)}) collective-permute-start(bf16[128,1536]{1,0:T(8,128)(2,1)S(1)} %copy-done), channel_id=1, source_target_pairs={{0,2},{1,3},{2,0},{3,1},{4,6},{5,7},{6,4},{7,5},{8,10},{9,11},{10,... | collective-permute-start | bytes 1179656 | tf_op jit(solution)/shard_map/ppermute | solution.py:27
  28.2 6.9 %collective-permute-done.8 = bf16[4,32,1536]{2,1,0:T(8,128)(2,1)S(1)} collective-permute-done((bf16[4,32,1536]{2,1,0:T(8,128)(2,1)S(1)}, bf16[4,32,1536]{2,1,0:T(8,128)(2,1)S(1)}, u32[]{:S(2)}, u32[]{:S(2)}) %collective-permute-start.8) | collective-permute-done | bytes 393248 | tf_op jit(solution)/shard_map/ppermute | solution.py:27
  37.5 1.2 %collective-permute-done.10 = bf16[4,4,32,1536]{3,2,0,1:T(8,128)(2,1)S(1)} collective-permute-done((bf16[4,4,32,1536]{3,2,0,1:T(8,128)(2,1)S(1)}, bf16[4,4,32,1536]{3,2,0,1:T(8,128)(2,1)S(1)}, u32[]{:S(2)}, u32[]{:S(2)}) %collective-permute-start.10) | collective-permute-done | bytes 1572896 | tf_op jit(solution)/shard_map/ppermute | solution.py:27
  38.9 0.8 collective-permute-done.6
  39.7 1.6 %collective-permute-start.11 = (bf16[128,1536]{1,0:T(8,128)(2,1)S(1)}, bf16[128,1536]{1,0:T(8,128)(2,1)S(1)}, u32[]{:S(2)}, u32[]{:S(2)}) collective-permute-start(bf16[128,1536]{1,0:T(8,128)(2,1)S(1)} %collective-permute-done.6), channel_id=1, source_target_pairs={{0,1},{1,2},{2,3},{3,0},{4,5},{5,6},{6,7},{7,4},{8,9},{9,10},{10,1... | collective-permute-start | bytes 1179656 | tf_op jit(solution)/shard_map/ppermute | solution.py:27
  41.3 1.7 %collective-permute-start.13 = (bf16[128,1536]{1,0:T(8,128)(2,1)S(1)}, bf16[128,1536]{1,0:T(8,128)(2,1)S(1)}, u32[]{:S(2)}, u32[]{:S(2)}) collective-permute-start(bf16[128,1536]{1,0:T(8,128)(2,1)S(1)} %collective-permute-done.6), channel_id=1, source_target_pairs={{0,3},{1,0},{2,1},{3,2},{4,7},{5,4},{6,5},{7,6},{8,11},{9,8},{10,9... | collective-permute-start | bytes 1179656 | tf_op jit(solution)/shard_map/ppermute | solution.py:27
  43.0 5.3 %convolution_convert_fusion.1 = bf16[1024,1536]{1,0:T(8,128)(2,1)S(1)} fusion(bf16[1024,1536]{1,0:T(8,128)(2,1)S(1)} %bitcast.102, bf16[1536,1536]{1,0:T(8,128)(2,1)S(1)} %bitcast.105), kind=kOutput, calls=%fused_computation.1 | convolution fusion | flops 4833411072 | bytes 11010048 | tf_op jit(solution)/shard_map/dot_general | solution.py:80
  48.8 5.4 %collective-permute-start.12 = (bf16[128,1536]{1,0:T(8,128)(2,1)S(1)}, bf16[128,1536]{1,0:T(8,128)(2,1)S(1)}, u32[]{:S(2)}, u32[]{:S(2)}) collective-permute-start(bf16[128,1536]{1,0:T(8,128)(2,1)S(1)} %collective-permute-done.2), channel_id=1, source_target_pairs={{0,4},{4,0},{1,5},{5,1},{2,6},{6,2},{3,7},{7,3},{8,12},{12,8},{9,1... | collective-permute-start | bytes 1179656 | tf_op jit(solution)/shard_map/ppermute | solution.py:27
  54.2 2.9 %collective-permute-start.18 = (bf16[128,1536]{1,0:T(8,128)(2,1)S(1)}, bf16[128,1536]{1,0:T(8,128)(2,1)S(1)}, u32[]{:S(2)}, u32[]{:S(2)}) collective-permute-start(bf16[128,1536]{1,0:T(8,128)(2,1)S(1)} %get-tuple-element.26), channel_id=1, source_target_pairs={{0,3},{1,0},{2,1},{3,2},{4,7},{5,4},{6,5},{7,6},{8,11},{9,8},{10,9... | collective-permute-start | bytes 1179656 | tf_op jit(solution)/shard_map/ppermute | solution.py:27
  57.5 2.7 %collective-permute-done.14 = bf16[128,1536]{1,0:T(8,128)(2,1)S(1)} collective-permute-done((bf16[128,1536]{1,0:T(8,128)(2,1)S(1)}, bf16[128,1536]{1,0:T(8,128)(2,1)S(1)}, u32[]{:S(2)}, u32[]{:S(2)}) %collective-permute-start.14) | collective-permute-done | bytes 393248 | tf_op jit(solution)/shard_map/ppermute | solution.py:27
  60.2 1.9 %collective-permute-start.19 = (bf16[128,1536]{1,0:T(8,128)(2,1)S(1)}, bf16[128,1536]{1,0:T(8,128)(2,1)S(1)}, u32[]{:S(2)}, u32[]{:S(2)}) collective-permute-start(bf16[128,1536]{1,0:T(8,128)(2,1)S(1)} %get-tuple-element.25), channel_id=1, source_target_pairs={{0,2},{1,3},{2,0},{3,1},{4,6},{5,7},{6,4},{7,5},{8,10},{9,11},{10,... | collective-permute-start | bytes 1179656 | tf_op jit(solution)/shard_map/ppermute | solution.py:27
  62.2 9.1 %collective-permute-done.12 = bf16[128,1536]{1,0:T(8,128)(2,1)S(1)} collective-permute-done((bf16[128,1536]{1,0:T(8,128)(2,1)S(1)}, bf16[128,1536]{1,0:T(8,128)(2,1)S(1)}, u32[]{:S(2)}, u32[]{:S(2)}) %collective-permute-start.12) | collective-permute-done | bytes 393248 | tf_op jit(solution)/shard_map/ppermute | solution.py:27
  71.4 1.4 %collective-permute-start.15 = (bf16[128,1536]{1,0:T(8,128)(2,1)S(1)}, bf16[128,1536]{1,0:T(8,128)(2,1)S(1)}, u32[]{:S(2)}, u32[]{:S(2)}) collective-permute-start(bf16[128,1536]{1,0:T(8,128)(2,1)S(1)} %get-tuple-element.27), channel_id=1, source_target_pairs={{0,1},{1,2},{2,3},{3,0},{4,5},{5,6},{6,7},{7,4},{8,9},{9,10},{10,1... | collective-permute-start | bytes 1179656 | tf_op jit(solution)/shard_map/ppermute | solution.py:27
  72.8 1.9 %collective-permute-start.16 = (bf16[128,1536]{1,0:T(8,128)(2,1)S(1)}, bf16[128,1536]{1,0:T(8,128)(2,1)S(1)}, u32[]{:S(2)}, u32[]{:S(2)}) collective-permute-start(bf16[128,1536]{1,0:T(8,128)(2,1)S(1)} %get-tuple-element.29), channel_id=1, source_target_pairs={{0,3},{1,0},{2,1},{3,2},{4,7},{5,4},{6,5},{7,6},{8,11},{9,8},{10,9... | collective-permute-start | bytes 1179656 | tf_op jit(solution)/shard_map/ppermute | solution.py:27
  74.7 1.4 %collective-permute-start.17 = (bf16[128,1536]{1,0:T(8,128)(2,1)S(1)}, bf16[128,1536]{1,0:T(8,128)(2,1)S(1)}, u32[]{:S(2)}, u32[]{:S(2)}) collective-permute-start(bf16[128,1536]{1,0:T(8,128)(2,1)S(1)} %get-tuple-element.28), channel_id=1, source_target_pairs={{0,2},{1,3},{2,0},{3,1},{4,6},{5,7},{6,4},{7,5},{8,10},{9,11},{10,... | collective-permute-start | bytes 1179656 | tf_op jit(solution)/shard_map/ppermute | solution.py:27
  76.3 5.5 %collective-permute-start.20 = (bf16[128,1536]{1,0:T(8,128)(2,1)S(1)}, bf16[128,1536]{1,0:T(8,128)(2,1)S(1)}, u32[]{:S(2)}, u32[]{:S(2)}) collective-permute-start(bf16[128,1536]{1,0:T(8,128)(2,1)S(1)} %fusion.48), channel_id=1, source_target_pairs={{0,4},{4,0},{1,5},{5,1},{2,6},{6,2},{3,7},{7,3},{8,12},{12,8},{9,1... | collective-permute-start | bytes 1179656 | tf_op jit(solution)/shard_map/ppermute | solution.py:27
  82.9 6.8 %convolution_convert_fusion = bf16[1536,1536]{1,0:T(8,128)(2,1)} fusion(bf16[1024,1536]{1,0:T(8,128)(2,1)S(1)} %bitcast.101, bf16[1024,1536]{1,0:T(8,128)(2,1)S(1)} %bitcast.103), kind=kOutput, calls=%fused_computation | convolution fusion | flops 4834197504 | bytes 11010048 | tf_op jit(solution)/shard_map/dot_general | solution.py:96
  89.7 1.5 %collective-permute-done.16 = bf16[128,1536]{1,0:T(8,128)(2,1)S(1)} collective-permute-done((bf16[128,1536]{1,0:T(8,128)(2,1)S(1)}, bf16[128,1536]{1,0:T(8,128)(2,1)S(1)}, u32[]{:S(2)}, u32[]{:S(2)}) %collective-permute-start.16) | collective-permute-done | bytes 393248 | tf_op jit(solution)/shard_map/ppermute | solution.py:27
  91.2 1.8 %collective-permute-done.17 = bf16[128,1536]{1,0:T(8,128)(2,1)S(1)} collective-permute-done((bf16[128,1536]{1,0:T(8,128)(2,1)S(1)}, bf16[128,1536]{1,0:T(8,128)(2,1)S(1)}, u32[]{:S(2)}, u32[]{:S(2)}) %collective-permute-start.17) | collective-permute-done | bytes 393248 | tf_op jit(solution)/shard_map/ppermute | solution.py:27
  93.0 1.8 %collective-permute-done.20 = bf16[128,1536]{1,0:T(8,128)(2,1)S(1)} collective-permute-done((bf16[128,1536]{1,0:T(8,128)(2,1)S(1)}, bf16[128,1536]{1,0:T(8,128)(2,1)S(1)}, u32[]{:S(2)}, u32[]{:S(2)}) %collective-permute-start.20) | collective-permute-done | bytes 393248 | tf_op jit(solution)/shard_map/ppermute | solution.py:27
  94.8 1.5 %fusion.7 = bf16[128,1536]{1,0:T(8,128)(2,1)} fusion(bf16[128,1536]{1,0:T(8,128)(2,1)S(1)} %copy-done, bf16[128,1536]{1,0:T(8,128)(2,1)S(1)} %collective-permute-done.20, bf16[128,1536]{1,0:T(8,128)(2,1)S(1)} %collective-permute-done.17, bf16[128,1536]{1,0:T(8,128)(2,1)S(1)} %collective-permute-done.16, bf16[128,1536]{1,0:T(8,128)(2,1)S(1)} %collective-permute-done.15, ...), kind=kLoop, calls=%fused_computation.56 | loop fusion | flops 5701632 | bytes 2752520 | tf_op jit(solution)/shard_map/convert_element_type | solution.py:100
  (52 shorter events, 5.9 us)
Async XLA Ops:
  0.6 9.1 %copy-start.1 = (bf16[32,1536]{1,0:T(8,128)(2,1)S(1)}, bf16[32,1536]{1,0:T(8,128)(2,1)}, u32[]{:S(2)}) copy-start(bf16[32,1536]{1,0:T(8,128)(2,1)} %param.3) | copy-start | bytes 294916
  0.6 8.7 %copy-start = (bf16[128,1536]{1,0:T(8,128)(2,1)S(1)}, bf16[128,1536]{1,0:T(8,128)(2,1)}, u32[]{:S(2)}) copy-start(bf16[128,1536]{1,0:T(8,128)(2,1)} %param.4) | copy-start | bytes 1179652
  0.6 9.2 %collective-permute-start.3 = (bf16[32,1536]{1,0:T(8,128)(2,1)}, bf16[32,1536]{1,0:T(8,128)(2,1)S(1)}, u32[]{:S(2)}, u32[]{:S(2)}) collective-permute-start(bf16[32,1536]{1,0:T(8,128)(2,1)} %param.3), channel_id=1, source_target_pairs={{0,64},{64,128},{128,192},{192,0},{1,65},{65,129},{129,193},{193,1... | collective-permute-start | bytes 294920 | tf_op jit(solution)/shard_map/ppermute | solution.py:27
  2.6 8.8 %collective-permute-start.4 = (bf16[32,1536]{1,0:T(8,128)(2,1)}, bf16[32,1536]{1,0:T(8,128)(2,1)S(1)}, u32[]{:S(2)}, u32[]{:S(2)}) collective-permute-start(bf16[32,1536]{1,0:T(8,128)(2,1)} %param.3), channel_id=1, source_target_pairs={{0,128},{64,192},{128,0},{192,64},{1,129},{65,193},{129,1},{193,65... | collective-permute-start | bytes 294920 | tf_op jit(solution)/shard_map/ppermute | solution.py:27
  4.9 8.5 %collective-permute-start.5 = (bf16[32,1536]{1,0:T(8,128)(2,1)}, bf16[32,1536]{1,0:T(8,128)(2,1)S(1)}, u32[]{:S(2)}, u32[]{:S(2)}) collective-permute-start(bf16[32,1536]{1,0:T(8,128)(2,1)} %param.3), channel_id=1, source_target_pairs={{0,192},{64,0},{128,64},{192,128},{1,193},{65,1},{129,65},{193,129... | collective-permute-start | bytes 294920 | tf_op jit(solution)/shard_map/ppermute | solution.py:27
  6.0 16.8 %collective-permute-start = (bf16[128,1536]{1,0:T(8,128)(2,1)}, bf16[128,1536]{1,0:T(8,128)(2,1)S(1)}, u32[]{:S(2)}, u32[]{:S(2)}) collective-permute-start(bf16[128,1536]{1,0:T(8,128)(2,1)} %param.4), channel_id=1, source_target_pairs={{0,1},{1,2},{2,3},{3,0},{4,5},{5,6},{6,7},{7,4},{8,9},{9,10},{10,1... | collective-permute-start | bytes 1179656 | tf_op jit(solution)/shard_map/ppermute | solution.py:27
  7.6 17.1 %collective-permute-start.1 = (bf16[128,1536]{1,0:T(8,128)(2,1)}, bf16[128,1536]{1,0:T(8,128)(2,1)S(1)}, u32[]{:S(2)}, u32[]{:S(2)}) collective-permute-start(bf16[128,1536]{1,0:T(8,128)(2,1)} %param.4), channel_id=1, source_target_pairs={{0,3},{1,0},{2,1},{3,2},{4,7},{5,4},{6,5},{7,6},{8,11},{9,8},{10,9... | collective-permute-start | bytes 1179656 | tf_op jit(solution)/shard_map/ppermute | solution.py:27
  13.4 14.8 %collective-permute-start.7 = (bf16[4,32,1536]{2,1,0:T(8,128)(2,1)S(1)}, bf16[4,32,1536]{2,1,0:T(8,128)(2,1)S(1)}, u32[]{:S(2)}, u32[]{:S(2)}) collective-permute-start(bf16[4,32,1536]{2,1,0:T(8,128)(2,1)S(1)} %bitcast_dynamic-update-slice_fusion.8), channel_id=1, source_target_pairs={{0,16},{16,32},{32,48},{48,0},{1,17},{17,33},{33,49},{49,1},{2,18}... | collective-permute-start | bytes 1179656 | tf_op jit(solution)/shard_map/ppermute | solution.py:27
  14.9 20.2 %collective-permute-start.9 = (bf16[4,32,1536]{2,1,0:T(8,128)(2,1)S(1)}, bf16[4,32,1536]{2,1,0:T(8,128)(2,1)S(1)}, u32[]{:S(2)}, u32[]{:S(2)}) collective-permute-start(bf16[4,32,1536]{2,1,0:T(8,128)(2,1)S(1)} %bitcast_dynamic-update-slice_fusion.8), channel_id=1, source_target_pairs={{0,48},{16,0},{32,16},{48,32},{1,49},{17,1},{33,17},{49,33},{2,50}... | collective-permute-start | bytes 1179656 | tf_op jit(solution)/shard_map/ppermute | solution.py:27
  16.7 23.0 %collective-permute-start.6 = (bf16[128,1536]{1,0:T(8,128)(2,1)S(1)}, bf16[128,1536]{1,0:T(8,128)(2,1)S(1)}, u32[]{:S(2)}, u32[]{:S(2)}) collective-permute-start(bf16[128,1536]{1,0:T(8,128)(2,1)S(1)} %copy-done), channel_id=1, source_target_pairs={{0,4},{4,0},{1,5},{5,1},{2,6},{6,2},{3,7},{7,3},{8,12},{12,8},{9,1... | collective-permute-start | bytes 1179656 | tf_op jit(solution)/shard_map/ppermute | solution.py:27
  22.8 12.3 %collective-permute-start.8 = (bf16[4,32,1536]{2,1,0:T(8,128)(2,1)S(1)}, bf16[4,32,1536]{2,1,0:T(8,128)(2,1)S(1)}, u32[]{:S(2)}, u32[]{:S(2)}) collective-permute-start(bf16[4,32,1536]{2,1,0:T(8,128)(2,1)S(1)} %bitcast_dynamic-update-slice_fusion.8), channel_id=1, source_target_pairs={{0,32},{16,48},{32,0},{48,16},{1,33},{17,49},{33,1},{49,17},{2,34}... | collective-permute-start | bytes 1179656 | tf_op jit(solution)/shard_map/ppermute | solution.py:27
  24.7 11.3 %collective-permute-start.2 = (bf16[128,1536]{1,0:T(8,128)(2,1)S(1)}, bf16[128,1536]{1,0:T(8,128)(2,1)S(1)}, u32[]{:S(2)}, u32[]{:S(2)}) collective-permute-start(bf16[128,1536]{1,0:T(8,128)(2,1)S(1)} %copy-done), channel_id=1, source_target_pairs={{0,2},{1,3},{2,0},{3,1},{4,6},{5,7},{6,4},{7,5},{8,10},{9,11},{10,... | collective-permute-start | bytes 1179656 | tf_op jit(solution)/shard_map/ppermute | solution.py:27
  35.2 3.5 %collective-permute-start.10 = (bf16[4,4,32,1536]{3,2,0,1:T(8,128)(2,1)S(1)}, bf16[4,4,32,1536]{3,2,0,1:T(8,128)(2,1)S(1)}, u32[]{:S(2)}, u32[]{:S(2)}) collective-permute-start(bf16[4,4,32,1536]{3,2,0,1:T(8,128)(2,1)S(1)} %bitcast_dynamic-update-slice_fusion.7), channel_id=1, source_target_pairs={{0,8},{8,0},{1,9},{9,1},{2,10},{10,2},{3,11},{11,3},{4,12},{12,4},... | collective-permute-start | bytes 4718600 | tf_op jit(solution)/shard_map/ppermute | solution.py:27
  36.5 6.4 %slice-start = ((s8[4718592]{0:T(1024)(128)(4,1)}), s8[4194304]{0:T(1024)(128)(4,1)S(1)}, s32[]{:S(2)}) async-start(s8[4718592]{0:T(1024)(128)(4,1)} %bitcast.104), calls=%async_computation | async-start | bytes 8388608
  36.9 6.0 %slice-start.1 = ((s8[4718592]{0:T(1024)(128)(4,1)}), s8[524288]{0:T(1024)(128)(4,1)S(1)}, s32[]{:S(2)}) async-start(s8[4718592]{0:T(1024)(128)(4,1)} %bitcast.104), calls=%async_computation.1 | async-start | bytes 1048576
  39.7 31.6 %collective-permute-start.11 = (bf16[128,1536]{1,0:T(8,128)(2,1)S(1)}, bf16[128,1536]{1,0:T(8,128)(2,1)S(1)}, u32[]{:S(2)}, u32[]{:S(2)}) collective-permute-start(bf16[128,1536]{1,0:T(8,128)(2,1)S(1)} %collective-permute-done.6), channel_id=1, source_target_pairs={{0,1},{1,2},{2,3},{3,0},{4,5},{5,6},{6,7},{7,4},{8,9},{9,10},{10,1... | collective-permute-start | bytes 1179656 | tf_op jit(solution)/shard_map/ppermute | solution.py:27
  41.3 30.0 %collective-permute-start.13 = (bf16[128,1536]{1,0:T(8,128)(2,1)S(1)}, bf16[128,1536]{1,0:T(8,128)(2,1)S(1)}, u32[]{:S(2)}, u32[]{:S(2)}) collective-permute-start(bf16[128,1536]{1,0:T(8,128)(2,1)S(1)} %collective-permute-done.6), channel_id=1, source_target_pairs={{0,3},{1,0},{2,1},{3,2},{4,7},{5,4},{6,5},{7,6},{8,11},{9,8},{10,9... | collective-permute-start | bytes 1179656 | tf_op jit(solution)/shard_map/ppermute | solution.py:27
  48.4 11.8 %collective-permute-start.14 = (bf16[128,1536]{1,0:T(8,128)(2,1)S(1)}, bf16[128,1536]{1,0:T(8,128)(2,1)S(1)}, u32[]{:S(2)}, u32[]{:S(2)}) collective-permute-start(bf16[128,1536]{1,0:T(8,128)(2,1)S(1)} %get-tuple-element.24), channel_id=1, source_target_pairs={{0,1},{1,2},{2,3},{3,0},{4,5},{5,6},{6,7},{7,4},{8,9},{9,10},{10,1... | collective-permute-start | bytes 1179656 | tf_op jit(solution)/shard_map/ppermute | solution.py:27
  48.8 22.5 %collective-permute-start.12 = (bf16[128,1536]{1,0:T(8,128)(2,1)S(1)}, bf16[128,1536]{1,0:T(8,128)(2,1)S(1)}, u32[]{:S(2)}, u32[]{:S(2)}) collective-permute-start(bf16[128,1536]{1,0:T(8,128)(2,1)S(1)} %collective-permute-done.2), channel_id=1, source_target_pairs={{0,4},{4,0},{1,5},{5,1},{2,6},{6,2},{3,7},{7,3},{8,12},{12,8},{9,1... | collective-permute-start | bytes 1179656 | tf_op jit(solution)/shard_map/ppermute | solution.py:27
  54.2 21.9 %collective-permute-start.18 = (bf16[128,1536]{1,0:T(8,128)(2,1)S(1)}, bf16[128,1536]{1,0:T(8,128)(2,1)S(1)}, u32[]{:S(2)}, u32[]{:S(2)}) collective-permute-start(bf16[128,1536]{1,0:T(8,128)(2,1)S(1)} %get-tuple-element.26), channel_id=1, source_target_pairs={{0,3},{1,0},{2,1},{3,2},{4,7},{5,4},{6,5},{7,6},{8,11},{9,8},{10,9... | collective-permute-start | bytes 1179656 | tf_op jit(solution)/shard_map/ppermute | solution.py:27
  60.2 15.9 %collective-permute-start.19 = (bf16[128,1536]{1,0:T(8,128)(2,1)S(1)}, bf16[128,1536]{1,0:T(8,128)(2,1)S(1)}, u32[]{:S(2)}, u32[]{:S(2)}) collective-permute-start(bf16[128,1536]{1,0:T(8,128)(2,1)S(1)} %get-tuple-element.25), channel_id=1, source_target_pairs={{0,2},{1,3},{2,0},{3,1},{4,6},{5,7},{6,4},{7,5},{8,10},{9,11},{10,... | collective-permute-start | bytes 1179656 | tf_op jit(solution)/shard_map/ppermute | solution.py:27
  71.4 18.3 %collective-permute-start.15 = (bf16[128,1536]{1,0:T(8,128)(2,1)S(1)}, bf16[128,1536]{1,0:T(8,128)(2,1)S(1)}, u32[]{:S(2)}, u32[]{:S(2)}) collective-permute-start(bf16[128,1536]{1,0:T(8,128)(2,1)S(1)} %get-tuple-element.27), channel_id=1, source_target_pairs={{0,1},{1,2},{2,3},{3,0},{4,5},{5,6},{6,7},{7,4},{8,9},{9,10},{10,1... | collective-permute-start | bytes 1179656 | tf_op jit(solution)/shard_map/ppermute | solution.py:27
  72.8 18.4 %collective-permute-start.16 = (bf16[128,1536]{1,0:T(8,128)(2,1)S(1)}, bf16[128,1536]{1,0:T(8,128)(2,1)S(1)}, u32[]{:S(2)}, u32[]{:S(2)}) collective-permute-start(bf16[128,1536]{1,0:T(8,128)(2,1)S(1)} %get-tuple-element.29), channel_id=1, source_target_pairs={{0,3},{1,0},{2,1},{3,2},{4,7},{5,4},{6,5},{7,6},{8,11},{9,8},{10,9... | collective-permute-start | bytes 1179656 | tf_op jit(solution)/shard_map/ppermute | solution.py:27
  74.7 18.3 %collective-permute-start.17 = (bf16[128,1536]{1,0:T(8,128)(2,1)S(1)}, bf16[128,1536]{1,0:T(8,128)(2,1)S(1)}, u32[]{:S(2)}, u32[]{:S(2)}) collective-permute-start(bf16[128,1536]{1,0:T(8,128)(2,1)S(1)} %get-tuple-element.28), channel_id=1, source_target_pairs={{0,2},{1,3},{2,0},{3,1},{4,6},{5,7},{6,4},{7,5},{8,10},{9,11},{10,... | collective-permute-start | bytes 1179656 | tf_op jit(solution)/shard_map/ppermute | solution.py:27
  76.3 18.5 %collective-permute-start.20 = (bf16[128,1536]{1,0:T(8,128)(2,1)S(1)}, bf16[128,1536]{1,0:T(8,128)(2,1)S(1)}, u32[]{:S(2)}, u32[]{:S(2)}) collective-permute-start(bf16[128,1536]{1,0:T(8,128)(2,1)S(1)} %fusion.48), channel_id=1, source_target_pairs={{0,4},{4,0},{1,5},{5,1},{2,6},{6,2},{3,7},{7,3},{8,12},{12,8},{9,1... | collective-permute-start | bytes 1179656 | tf_op jit(solution)/shard_map/ppermute | solution.py:27

commit v5 on v4

--- a/solution.py
+++ b/solution.py
@@ -74,7 +74,7 @@
 
     gc = place([gx, send(after(gx, own1, own3), "c", 1)], c, 2)
     turn = after(swapped, gc)
-    far1, far3 = (send(turn, "y", k) for k in (1, 3))
+    far1 = send(turn, "y", 1)
     far2 = send(after(own2, gc, swapped), "zh", 1)
     grads = gc.transpose(2, 1, 0, 3, 4).reshape(8 * tok, width)
     sums = lax.dot_general(grads, weight, (((1,), (1,)), ((), ())), preferred_element_type=jnp.float32)
@@ -85,7 +85,8 @@
     p_ready = p_other
     r_other = [send(for_y(p_ready, k), "y", k) for k in (1, 3, 2)]
 
-    p_ready = after(p_mine, far1, far3, far2, r_other[0])
+    far3 = send(after(swapped, r_other[0]), "y", 3)
+    p_ready = after(p_mine, far1, far2, r_other[0])
     r_mine = [send(for_y(p_ready, k), "y", k) for k in (1, 3, 2)]
     s_other = send(add_up(p_other, r_other).astype(jnp.bfloat16), "zh", 1)
 

time: 96.4 us -> 108 us (1.12)
  waiting for transfers between devices: 29.9 us -> 38.6 us
  starting transfers between devices: 47.1 us -> 49.6 us
    ppermute x21, waiting for transfers between devices: 29.9 us -> 38.6 us  [send(): return lax.ppermute(v, axis, [(i, (i + step) % n) for i in range(n)])]
    ppermute x21, starting transfers between devices: 47.1 us -> 49.6 us  [send(): return lax.ppermute(v, axis, [(i, (i + step) % n) for i in range(n)])]
  transfers between devices with their start and end apart: 21 -> 21, of which waited for: 11 -> 8; matrix products, arithmetic and copies ran while one was open for 17% -> 16% of each run, Pallas kernels for 0% -> 0%
where the time goes in v5:
time: 108 us
  starting transfers between devices  49.6 us (46%)
  waiting for transfers between devices  38.6 us (36%)
  matrix products  12.1 us (11%)
  other arithmetic  4 us (4%)
  local copies, waits for them, and re-layouts  2.19 us (2%)
    ppermute x21, starting transfers between devices, send(): return lax.ppermute(v, axis, [(i, (i + step) % n) for i in range(n)])  49.6 us
    ppermute x21, waiting for transfers between devices, send(): return lax.ppermute(v, axis, [(i, (i + step) % n) for i in range(n)])  38.6 us
    dot_general x1, matrix products, body(): lax.dot_general(activated, grads, (((0,), (0,)), ((), ())), preferred_ele...  6.8 us
    dot_general x1, matrix products, body(): lax.dot_general(grads, weight, (((1,), (1,)), ((), ())), preferred_elemen...  5.28 us
    dynamic_update_slice x8, other arithmetic, act(): out = lax.dynamic_update_index_in_dim(out, a, lax.rem(y + (4 - k), 4), 0)  2.27 us
  transfers between devices with their start and end apart: 21, of which 8 were waited for; matrix products, arithmetic and copies ran while one was open for 16% of the time, Pallas kernels for 0%

profile of v5, /device:TPU:32, one launch (start us, length us, event | category | flops | bytes accessed | tf_op | source)
XLA Modules:
  0.0 107.5 jit_solution(1703471972059907165)
XLA Ops:
  0.6 2.0 %collective-permute-start.3 = (bf16[32,1536]{1,0:T(8,128)(2,1)}, bf16[32,1536]{1,0:T(8,128)(2,1)S(1)}, u32[]{:S(2)}, u32[]{:S(2)}) collective-permute-start(bf16[32,1536]{1,0:T(8,128)(2,1)} %param.3), channel_id=1, source_target_pairs={{0,64},{64,128},{128,192},{192,0},{1,65},{65,129},{129,193},{193,1... | collective-permute-start | bytes 294920 | tf_op jit(solution)/shard_map/ppermute | solution.py:27
  2.6 2.3 %collective-permute-start.4 = (bf16[32,1536]{1,0:T(8,128)(2,1)}, bf16[32,1536]{1,0:T(8,128)(2,1)S(1)}, u32[]{:S(2)}, u32[]{:S(2)}) collective-permute-start(bf16[32,1536]{1,0:T(8,128)(2,1)} %param.3), channel_id=1, source_target_pairs={{0,128},{64,192},{128,0},{192,64},{1,129},{65,193},{129,1},{193,65... | collective-permute-start | bytes 294920 | tf_op jit(solution)/shard_map/ppermute | solution.py:27
  4.9 1.1 %collective-permute-start.5 = (bf16[32,1536]{1,0:T(8,128)(2,1)}, bf16[32,1536]{1,0:T(8,128)(2,1)S(1)}, u32[]{:S(2)}, u32[]{:S(2)}) collective-permute-start(bf16[32,1536]{1,0:T(8,128)(2,1)} %param.3), channel_id=1, source_target_pairs={{0,192},{64,0},{128,64},{192,128},{1,193},{65,1},{129,65},{193,129... | collective-permute-start | bytes 294920 | tf_op jit(solution)/shard_map/ppermute | solution.py:27
  6.0 1.6 %collective-permute-start = (bf16[128,1536]{1,0:T(8,128)(2,1)}, bf16[128,1536]{1,0:T(8,128)(2,1)S(1)}, u32[]{:S(2)}, u32[]{:S(2)}) collective-permute-start(bf16[128,1536]{1,0:T(8,128)(2,1)} %param.4), channel_id=1, source_target_pairs={{0,1},{1,2},{2,3},{3,0},{4,5},{5,6},{6,7},{7,4},{8,9},{9,10},{10,1... | collective-permute-start | bytes 1179656 | tf_op jit(solution)/shard_map/ppermute | solution.py:27
  7.6 1.7 %collective-permute-start.1 = (bf16[128,1536]{1,0:T(8,128)(2,1)}, bf16[128,1536]{1,0:T(8,128)(2,1)S(1)}, u32[]{:S(2)}, u32[]{:S(2)}) collective-permute-start(bf16[128,1536]{1,0:T(8,128)(2,1)} %param.4), channel_id=1, source_target_pairs={{0,3},{1,0},{2,1},{3,2},{4,7},{5,4},{6,5},{7,6},{8,11},{9,8},{10,9... | collective-permute-start | bytes 1179656 | tf_op jit(solution)/shard_map/ppermute | solution.py:27
  9.9 1.5 %collective-permute-done.4 = bf16[32,1536]{1,0:T(8,128)(2,1)S(1)} collective-permute-done((bf16[32,1536]{1,0:T(8,128)(2,1)}, bf16[32,1536]{1,0:T(8,128)(2,1)S(1)}, u32[]{:S(2)}, u32[]{:S(2)}) %collective-permute-start.4) | collective-permute-done | bytes 98336 | tf_op jit(solution)/shard_map/ppermute | solution.py:27
  11.4 2.0 %collective-permute-done.5 = bf16[32,1536]{1,0:T(8,128)(2,1)S(1)} collective-permute-done((bf16[32,1536]{1,0:T(8,128)(2,1)}, bf16[32,1536]{1,0:T(8,128)(2,1)S(1)}, u32[]{:S(2)}, u32[]{:S(2)}) %collective-permute-start.5) | collective-permute-done | bytes 98336 | tf_op jit(solution)/shard_map/ppermute | solution.py:27
  13.4 1.5 %collective-permute-start.7 = (bf16[4,32,1536]{2,1,0:T(8,128)(2,1)S(1)}, bf16[4,32,1536]{2,1,0:T(8,128)(2,1)S(1)}, u32[]{:S(2)}, u32[]{:S(2)}) collective-permute-start(bf16[4,32,1536]{2,1,0:T(8,128)(2,1)S(1)} %bitcast_dynamic-update-slice_fusion.8), channel_id=1, source_target_pairs={{0,16},{16,32},{32,48},{48,0},{1,17},{17,33},{33,49},{49,1},{2,18}... | collective-permute-start | bytes 1179656 | tf_op jit(solution)/shard_map/ppermute | solution.py:27
  14.9 1.8 %collective-permute-start.9 = (bf16[4,32,1536]{2,1,0:T(8,128)(2,1)S(1)}, bf16[4,32,1536]{2,1,0:T(8,128)(2,1)S(1)}, u32[]{:S(2)}, u32[]{:S(2)}) collective-permute-start(bf16[4,32,1536]{2,1,0:T(8,128)(2,1)S(1)} %bitcast_dynamic-update-slice_fusion.8), channel_id=1, source_target_pairs={{0,48},{16,0},{32,16},{48,32},{1,49},{17,1},{33,17},{49,33},{2,50}... | collective-permute-start | bytes 1179656 | tf_op jit(solution)/shard_map/ppermute | solution.py:27
  16.7 5.9 %collective-permute-start.6 = (bf16[128,1536]{1,0:T(8,128)(2,1)S(1)}, bf16[128,1536]{1,0:T(8,128)(2,1)S(1)}, u32[]{:S(2)}, u32[]{:S(2)}) collective-permute-start(bf16[128,1536]{1,0:T(8,128)(2,1)S(1)} %copy-done), channel_id=1, source_target_pairs={{0,4},{4,0},{1,5},{5,1},{2,6},{6,2},{3,7},{7,3},{8,12},{12,8},{9,1... | collective-permute-start | bytes 1179656 | tf_op jit(solution)/shard_map/ppermute | solution.py:27
  22.8 1.9 %collective-permute-start.8 = (bf16[4,32,1536]{2,1,0:T(8,128)(2,1)S(1)}, bf16[4,32,1536]{2,1,0:T(8,128)(2,1)S(1)}, u32[]{:S(2)}, u32[]{:S(2)}) collective-permute-start(bf16[4,32,1536]{2,1,0:T(8,128)(2,1)S(1)} %bitcast_dynamic-update-slice_fusion.8), channel_id=1, source_target_pairs={{0,32},{16,48},{32,0},{48,16},{1,33},{17,49},{33,1},{49,17},{2,34}... | collective-permute-start | bytes 1179656 | tf_op jit(solution)/shard_map/ppermute | solution.py:27
  24.7 3.2 %collective-permute-start.2 = (bf16[128,1536]{1,0:T(8,128)(2,1)S(1)}, bf16[128,1536]{1,0:T(8,128)(2,1)S(1)}, u32[]{:S(2)}, u32[]{:S(2)}) collective-permute-start(bf16[128,1536]{1,0:T(8,128)(2,1)S(1)} %copy-done), channel_id=1, source_target_pairs={{0,2},{1,3},{2,0},{3,1},{4,6},{5,7},{6,4},{7,5},{8,10},{9,11},{10,... | collective-permute-start | bytes 1179656 | tf_op jit(solution)/shard_map/ppermute | solution.py:27
  28.2 6.9 %collective-permute-done.8 = bf16[4,32,1536]{2,1,0:T(8,128)(2,1)S(1)} collective-permute-done((bf16[4,32,1536]{2,1,0:T(8,128)(2,1)S(1)}, bf16[4,32,1536]{2,1,0:T(8,128)(2,1)S(1)}, u32[]{:S(2)}, u32[]{:S(2)}) %collective-permute-start.8) | collective-permute-done | bytes 393248 | tf_op jit(solution)/shard_map/ppermute | solution.py:27
  35.3 0.7 collective-permute-done.2
  37.0 0.3 broadcast_in_dim.88
  37.5 1.2 %collective-permute-done.10 = bf16[4,4,32,1536]{3,2,0,1:T(8,128)(2,1)S(1)} collective-permute-done((bf16[4,4,32,1536]{3,2,0,1:T(8,128)(2,1)S(1)}, bf16[4,4,32,1536]{3,2,0,1:T(8,128)(2,1)S(1)}, u32[]{:S(2)}, u32[]{:S(2)}) %collective-permute-start.10) | collective-permute-done | bytes 1572896 | tf_op jit(solution)/shard_map/ppermute | solution.py:27
  38.9 5.3 %convolution_convert_fusion.1 = bf16[1024,1536]{1,0:T(8,128)(2,1)S(1)} fusion(bf16[1024,1536]{1,0:T(8,128)(2,1)S(1)} %bitcast.102, bf16[1536,1536]{1,0:T(8,128)(2,1)S(1)} %bitcast.105), kind=kOutput, calls=%fused_computation.1 | convolution fusion | flops 4833411072 | bytes 11010048 | tf_op jit(solution)/shard_map/dot_general | solution.py:80
  44.3 1.8 %collective-permute-start.13 = (bf16[128,1536]{1,0:T(8,128)(2,1)S(1)}, bf16[128,1536]{1,0:T(8,128)(2,1)S(1)}, u32[]{:S(2)}, u32[]{:S(2)}) collective-permute-start(bf16[128,1536]{1,0:T(8,128)(2,1)S(1)} %get-tuple-element.28), channel_id=1, source_target_pairs={{0,1},{1,2},{2,3},{3,0},{4,5},{5,6},{6,7},{7,4},{8,9},{9,10},{10,1... | collective-permute-start | bytes 1179656 | tf_op jit(solution)/shard_map/ppermute | solution.py:27
  46.2 5.7 %collective-permute-start.12 = (bf16[128,1536]{1,0:T(8,128)(2,1)S(1)}, bf16[128,1536]{1,0:T(8,128)(2,1)S(1)}, u32[]{:S(2)}, u32[]{:S(2)}) collective-permute-start(bf16[128,1536]{1,0:T(8,128)(2,1)S(1)} %collective-permute-done.2), channel_id=1, source_target_pairs={{0,4},{4,0},{1,5},{5,1},{2,6},{6,2},{3,7},{7,3},{8,12},{12,8},{9,1... | collective-permute-start | bytes 1179656 | tf_op jit(solution)/shard_map/ppermute | solution.py:27
  51.9 1.6 %collective-permute-start.11 = (bf16[128,1536]{1,0:T(8,128)(2,1)S(1)}, bf16[128,1536]{1,0:T(8,128)(2,1)S(1)}, u32[]{:S(2)}, u32[]{:S(2)}) collective-permute-start(bf16[128,1536]{1,0:T(8,128)(2,1)S(1)} %collective-permute-done.6), channel_id=1, source_target_pairs={{0,1},{1,2},{2,3},{3,0},{4,5},{5,6},{6,7},{7,4},{8,9},{9,10},{10,1... | collective-permute-start | bytes 1179656 | tf_op jit(solution)/shard_map/ppermute | solution.py:27
  53.5 1.7 %collective-permute-start.18 = (bf16[128,1536]{1,0:T(8,128)(2,1)S(1)}, bf16[128,1536]{1,0:T(8,128)(2,1)S(1)}, u32[]{:S(2)}, u32[]{:S(2)}) collective-permute-start(bf16[128,1536]{1,0:T(8,128)(2,1)S(1)} %get-tuple-element.26), channel_id=1, source_target_pairs={{0,3},{1,0},{2,1},{3,2},{4,7},{5,4},{6,5},{7,6},{8,11},{9,8},{10,9... | collective-permute-start | bytes 1179656 | tf_op jit(solution)/shard_map/ppermute | solution.py:27
  55.1 1.7 %collective-permute-start.19 = (bf16[128,1536]{1,0:T(8,128)(2,1)S(1)}, bf16[128,1536]{1,0:T(8,128)(2,1)S(1)}, u32[]{:S(2)}, u32[]{:S(2)}) collective-permute-start(bf16[128,1536]{1,0:T(8,128)(2,1)S(1)} %get-tuple-element.27), channel_id=1, source_target_pairs={{0,2},{1,3},{2,0},{3,1},{4,6},{5,7},{6,4},{7,5},{8,10},{9,11},{10,... | collective-permute-start | bytes 1179656 | tf_op jit(solution)/shard_map/ppermute | solution.py:27
  57.4 0.4 collective-permute-done.13
  57.7 11.9 %collective-permute-done.12 = bf16[128,1536]{1,0:T(8,128)(2,1)S(1)} collective-permute-done((bf16[128,1536]{1,0:T(8,128)(2,1)S(1)}, bf16[128,1536]{1,0:T(8,128)(2,1)S(1)}, u32[]{:S(2)}, u32[]{:S(2)}) %collective-permute-start.12) | collective-permute-done | bytes 393248 | tf_op jit(solution)/shard_map/ppermute | solution.py:27
  69.7 1.7 %collective-permute-start.15 = (bf16[128,1536]{1,0:T(8,128)(2,1)S(1)}, bf16[128,1536]{1,0:T(8,128)(2,1)S(1)}, u32[]{:S(2)}, u32[]{:S(2)}) collective-permute-start(bf16[128,1536]{1,0:T(8,128)(2,1)S(1)} %get-tuple-element.29), channel_id=1, source_target_pairs={{0,1},{1,2},{2,3},{3,0},{4,5},{5,6},{6,7},{7,4},{8,9},{9,10},{10,1... | collective-permute-start | bytes 1179656 | tf_op jit(solution)/shard_map/ppermute | solution.py:27
  71.4 1.7 %collective-permute-start.16 = (bf16[128,1536]{1,0:T(8,128)(2,1)S(1)}, bf16[128,1536]{1,0:T(8,128)(2,1)S(1)}, u32[]{:S(2)}, u32[]{:S(2)}) collective-permute-start(bf16[128,1536]{1,0:T(8,128)(2,1)S(1)} %get-tuple-element.31), channel_id=1, source_target_pairs={{0,3},{1,0},{2,1},{3,2},{4,7},{5,4},{6,5},{7,6},{8,11},{9,8},{10,9... | collective-permute-start | bytes 1179656 | tf_op jit(solution)/shard_map/ppermute | solution.py:27
  73.0 4.5 %collective-permute-start.17 = (bf16[128,1536]{1,0:T(8,128)(2,1)S(1)}, bf16[128,1536]{1,0:T(8,128)(2,1)S(1)}, u32[]{:S(2)}, u32[]{:S(2)}) collective-permute-start(bf16[128,1536]{1,0:T(8,128)(2,1)S(1)} %get-tuple-element.30), channel_id=1, source_target_pairs={{0,2},{1,3},{2,0},{3,1},{4,6},{5,7},{6,4},{7,5},{8,10},{9,11},{10,... | collective-permute-start | bytes 1179656 | tf_op jit(solution)/shard_map/ppermute | solution.py:27
  77.8 5.7 %collective-permute-start.20 = (bf16[128,1536]{1,0:T(8,128)(2,1)S(1)}, bf16[128,1536]{1,0:T(8,128)(2,1)S(1)}, u32[]{:S(2)}, u32[]{:S(2)}) collective-permute-start(bf16[128,1536]{1,0:T(8,128)(2,1)S(1)} %fusion.48), channel_id=1, source_target_pairs={{0,4},{4,0},{1,5},{5,1},{2,6},{6,2},{3,7},{7,3},{8,12},{12,8},{9,1... | collective-permute-start | bytes 1179656 | tf_op jit(solution)/shard_map/ppermute | solution.py:27
  83.5 0.6 collective-permute-start.14
  84.7 14.1 %collective-permute-done.14 = bf16[128,1536]{1,0:T(8,128)(2,1)S(1)} collective-permute-done((bf16[128,1536]{1,0:T(8,128)(2,1)S(1)}, bf16[128,1536]{1,0:T(8,128)(2,1)S(1)}, u32[]{:S(2)}, u32[]{:S(2)}) %collective-permute-start.14) | collective-permute-done | bytes 393248 | tf_op jit(solution)/shard_map/ppermute | solution.py:27
  99.2 6.8 %convolution_convert_fusion = bf16[1536,1536]{1,0:T(8,128)(2,1)} fusion(bf16[1024,1536]{1,0:T(8,128)(2,1)S(1)} %bitcast.101, bf16[1024,1536]{1,0:T(8,128)(2,1)S(1)} %bitcast.103), kind=kOutput, calls=%fused_computation | convolution fusion | flops 4834197504 | bytes 11010048 | tf_op jit(solution)/shard_map/dot_general | solution.py:97
  106.0 1.5 %fusion.7 = bf16[128,1536]{1,0:T(8,128)(2,1)} fusion(bf16[128,1536]{1,0:T(8,128)(2,1)S(1)} %copy-done, bf16[128,1536]{1,0:T(8,128)(2,1)S(1)} %collective-permute-done.20, bf16[128,1536]{1,0:T(8,128)(2,1)S(1)} %collective-permute-done.17, bf16[128,1536]{1,0:T(8,128)(2,1)S(1)} %collective-permute-done.16, bf16[128,1536]{1,0:T(8,128)(2,1)S(1)} %collective-permute-done.15, ...), kind=kLoop, calls=%fused_computation.56 | loop fusion | flops 5701632 | bytes 2752520 | tf_op jit(solution)/shard_map/convert_element_type | solution.py:101
  (52 shorter events, 4.5 us)
Async XLA Ops:
  0.6 9.1 %copy-start.1 = (bf16[32,1536]{1,0:T(8,128)(2,1)S(1)}, bf16[32,1536]{1,0:T(8,128)(2,1)}, u32[]{:S(2)}) copy-start(bf16[32,1536]{1,0:T(8,128)(2,1)} %param.3) | copy-start | bytes 294916
  0.6 8.7 %copy-start = (bf16[128,1536]{1,0:T(8,128)(2,1)S(1)}, bf16[128,1536]{1,0:T(8,128)(2,1)}, u32[]{:S(2)}) copy-start(bf16[128,1536]{1,0:T(8,128)(2,1)} %param.4) | copy-start | bytes 1179652
  0.6 9.2 %collective-permute-start.3 = (bf16[32,1536]{1,0:T(8,128)(2,1)}, bf16[32,1536]{1,0:T(8,128)(2,1)S(1)}, u32[]{:S(2)}, u32[]{:S(2)}) collective-permute-start(bf16[32,1536]{1,0:T(8,128)(2,1)} %param.3), channel_id=1, source_target_pairs={{0,64},{64,128},{128,192},{192,0},{1,65},{65,129},{129,193},{193,1... | collective-permute-start | bytes 294920 | tf_op jit(solution)/shard_map/ppermute | solution.py:27
  2.6 8.8 %collective-permute-start.4 = (bf16[32,1536]{1,0:T(8,128)(2,1)}, bf16[32,1536]{1,0:T(8,128)(2,1)S(1)}, u32[]{:S(2)}, u32[]{:S(2)}) collective-permute-start(bf16[32,1536]{1,0:T(8,128)(2,1)} %param.3), channel_id=1, source_target_pairs={{0,128},{64,192},{128,0},{192,64},{1,129},{65,193},{129,1},{193,65... | collective-permute-start | bytes 294920 | tf_op jit(solution)/shard_map/ppermute | solution.py:27
  4.9 8.5 %collective-permute-start.5 = (bf16[32,1536]{1,0:T(8,128)(2,1)}, bf16[32,1536]{1,0:T(8,128)(2,1)S(1)}, u32[]{:S(2)}, u32[]{:S(2)}) collective-permute-start(bf16[32,1536]{1,0:T(8,128)(2,1)} %param.3), channel_id=1, source_target_pairs={{0,192},{64,0},{128,64},{192,128},{1,193},{65,1},{129,65},{193,129... | collective-permute-start | bytes 294920 | tf_op jit(solution)/shard_map/ppermute | solution.py:27
  6.0 16.8 %collective-permute-start = (bf16[128,1536]{1,0:T(8,128)(2,1)}, bf16[128,1536]{1,0:T(8,128)(2,1)S(1)}, u32[]{:S(2)}, u32[]{:S(2)}) collective-permute-start(bf16[128,1536]{1,0:T(8,128)(2,1)} %param.4), channel_id=1, source_target_pairs={{0,1},{1,2},{2,3},{3,0},{4,5},{5,6},{6,7},{7,4},{8,9},{9,10},{10,1... | collective-permute-start | bytes 1179656 | tf_op jit(solution)/shard_map/ppermute | solution.py:27
  7.6 17.1 %collective-permute-start.1 = (bf16[128,1536]{1,0:T(8,128)(2,1)}, bf16[128,1536]{1,0:T(8,128)(2,1)S(1)}, u32[]{:S(2)}, u32[]{:S(2)}) collective-permute-start(bf16[128,1536]{1,0:T(8,128)(2,1)} %param.4), channel_id=1, source_target_pairs={{0,3},{1,0},{2,1},{3,2},{4,7},{5,4},{6,5},{7,6},{8,11},{9,8},{10,9... | collective-permute-start | bytes 1179656 | tf_op jit(solution)/shard_map/ppermute | solution.py:27
  13.4 14.8 %collective-permute-start.7 = (bf16[4,32,1536]{2,1,0:T(8,128)(2,1)S(1)}, bf16[4,32,1536]{2,1,0:T(8,128)(2,1)S(1)}, u32[]{:S(2)}, u32[]{:S(2)}) collective-permute-start(bf16[4,32,1536]{2,1,0:T(8,128)(2,1)S(1)} %bitcast_dynamic-update-slice_fusion.8), channel_id=1, source_target_pairs={{0,16},{16,32},{32,48},{48,0},{1,17},{17,33},{33,49},{49,1},{2,18}... | collective-permute-start | bytes 1179656 | tf_op jit(solution)/shard_map/ppermute | solution.py:27
  14.9 20.2 %collective-permute-start.9 = (bf16[4,32,1536]{2,1,0:T(8,128)(2,1)S(1)}, bf16[4,32,1536]{2,1,0:T(8,128)(2,1)S(1)}, u32[]{:S(2)}, u32[]{:S(2)}) collective-permute-start(bf16[4,32,1536]{2,1,0:T(8,128)(2,1)S(1)} %bitcast_dynamic-update-slice_fusion.8), channel_id=1, source_target_pairs={{0,48},{16,0},{32,16},{48,32},{1,49},{17,1},{33,17},{49,33},{2,50}... | collective-permute-start | bytes 1179656 | tf_op jit(solution)/shard_map/ppermute | solution.py:27
  16.7 29.4 %collective-permute-start.6 = (bf16[128,1536]{1,0:T(8,128)(2,1)S(1)}, bf16[128,1536]{1,0:T(8,128)(2,1)S(1)}, u32[]{:S(2)}, u32[]{:S(2)}) collective-permute-start(bf16[128,1536]{1,0:T(8,128)(2,1)S(1)} %copy-done), channel_id=1, source_target_pairs={{0,4},{4,0},{1,5},{5,1},{2,6},{6,2},{3,7},{7,3},{8,12},{12,8},{9,1... | collective-permute-start | bytes 1179656 | tf_op jit(solution)/shard_map/ppermute | solution.py:27
  22.8 12.3 %collective-permute-start.8 = (bf16[4,32,1536]{2,1,0:T(8,128)(2,1)S(1)}, bf16[4,32,1536]{2,1,0:T(8,128)(2,1)S(1)}, u32[]{:S(2)}, u32[]{:S(2)}) collective-permute-start(bf16[4,32,1536]{2,1,0:T(8,128)(2,1)S(1)} %bitcast_dynamic-update-slice_fusion.8), channel_id=1, source_target_pairs={{0,32},{16,48},{32,0},{48,16},{1,33},{17,49},{33,1},{49,17},{2,34}... | collective-permute-start | bytes 1179656 | tf_op jit(solution)/shard_map/ppermute | solution.py:27
  24.7 11.3 %collective-permute-start.2 = (bf16[128,1536]{1,0:T(8,128)(2,1)S(1)}, bf16[128,1536]{1,0:T(8,128)(2,1)S(1)}, u32[]{:S(2)}, u32[]{:S(2)}) collective-permute-start(bf16[128,1536]{1,0:T(8,128)(2,1)S(1)} %copy-done), channel_id=1, source_target_pairs={{0,2},{1,3},{2,0},{3,1},{4,6},{5,7},{6,4},{7,5},{8,10},{9,11},{10,... | collective-permute-start | bytes 1179656 | tf_op jit(solution)/shard_map/ppermute | solution.py:27
  35.2 3.5 %collective-permute-start.10 = (bf16[4,4,32,1536]{3,2,0,1:T(8,128)(2,1)S(1)}, bf16[4,4,32,1536]{3,2,0,1:T(8,128)(2,1)S(1)}, u32[]{:S(2)}, u32[]{:S(2)}) collective-permute-start(bf16[4,4,32,1536]{3,2,0,1:T(8,128)(2,1)S(1)} %bitcast_dynamic-update-slice_fusion.7), channel_id=1, source_target_pairs={{0,8},{8,0},{1,9},{9,1},{2,10},{10,2},{3,11},{11,3},{4,12},{12,4},... | collective-permute-start | bytes 4718600 | tf_op jit(solution)/shard_map/ppermute | solution.py:27
  36.5 2.4 %slice-start = ((s8[4718592]{0:T(1024)(128)(4,1)}), s8[4194304]{0:T(1024)(128)(4,1)S(1)}, s32[]{:S(2)}) async-start(s8[4718592]{0:T(1024)(128)(4,1)} %bitcast.104), calls=%async_computation | async-start | bytes 8388608
  36.9 2.0 %slice-start.1 = ((s8[4718592]{0:T(1024)(128)(4,1)}), s8[524288]{0:T(1024)(128)(4,1)S(1)}, s32[]{:S(2)}) async-start(s8[4718592]{0:T(1024)(128)(4,1)} %bitcast.104), calls=%async_computation.1 | async-start | bytes 1048576
  44.3 13.4 %collective-permute-start.13 = (bf16[128,1536]{1,0:T(8,128)(2,1)S(1)}, bf16[128,1536]{1,0:T(8,128)(2,1)S(1)}, u32[]{:S(2)}, u32[]{:S(2)}) collective-permute-start(bf16[128,1536]{1,0:T(8,128)(2,1)S(1)} %get-tuple-element.28), channel_id=1, source_target_pairs={{0,1},{1,2},{2,3},{3,0},{4,5},{5,6},{6,7},{7,4},{8,9},{9,10},{10,1... | collective-permute-start | bytes 1179656 | tf_op jit(solution)/shard_map/ppermute | solution.py:27
  46.2 23.4 %collective-permute-start.12 = (bf16[128,1536]{1,0:T(8,128)(2,1)S(1)}, bf16[128,1536]{1,0:T(8,128)(2,1)S(1)}, u32[]{:S(2)}, u32[]{:S(2)}) collective-permute-start(bf16[128,1536]{1,0:T(8,128)(2,1)S(1)} %collective-permute-done.2), channel_id=1, source_target_pairs={{0,4},{4,0},{1,5},{5,1},{2,6},{6,2},{3,7},{7,3},{8,12},{12,8},{9,1... | collective-permute-start | bytes 1179656 | tf_op jit(solution)/shard_map/ppermute | solution.py:27
  51.9 17.7 %collective-permute-start.11 = (bf16[128,1536]{1,0:T(8,128)(2,1)S(1)}, bf16[128,1536]{1,0:T(8,128)(2,1)S(1)}, u32[]{:S(2)}, u32[]{:S(2)}) collective-permute-start(bf16[128,1536]{1,0:T(8,128)(2,1)S(1)} %collective-permute-done.6), channel_id=1, source_target_pairs={{0,1},{1,2},{2,3},{3,0},{4,5},{5,6},{6,7},{7,4},{8,9},{9,10},{10,1... | collective-permute-start | bytes 1179656 | tf_op jit(solution)/shard_map/ppermute | solution.py:27
  53.5 24.0 %collective-permute-start.18 = (bf16[128,1536]{1,0:T(8,128)(2,1)S(1)}, bf16[128,1536]{1,0:T(8,128)(2,1)S(1)}, u32[]{:S(2)}, u32[]{:S(2)}) collective-permute-start(bf16[128,1536]{1,0:T(8,128)(2,1)S(1)} %get-tuple-element.26), channel_id=1, source_target_pairs={{0,3},{1,0},{2,1},{3,2},{4,7},{5,4},{6,5},{7,6},{8,11},{9,8},{10,9... | collective-permute-start | bytes 1179656 | tf_op jit(solution)/shard_map/ppermute | solution.py:27
  55.1 22.4 %collective-permute-start.19 = (bf16[128,1536]{1,0:T(8,128)(2,1)S(1)}, bf16[128,1536]{1,0:T(8,128)(2,1)S(1)}, u32[]{:S(2)}, u32[]{:S(2)}) collective-permute-start(bf16[128,1536]{1,0:T(8,128)(2,1)S(1)} %get-tuple-element.27), channel_id=1, source_target_pairs={{0,2},{1,3},{2,0},{3,1},{4,6},{5,7},{6,4},{7,5},{8,10},{9,11},{10,... | collective-permute-start | bytes 1179656 | tf_op jit(solution)/shard_map/ppermute | solution.py:27
  69.7 36.3 %collective-permute-start.15 = (bf16[128,1536]{1,0:T(8,128)(2,1)S(1)}, bf16[128,1536]{1,0:T(8,128)(2,1)S(1)}, u32[]{:S(2)}, u32[]{:S(2)}) collective-permute-start(bf16[128,1536]{1,0:T(8,128)(2,1)S(1)} %get-tuple-element.29), channel_id=1, source_target_pairs={{0,1},{1,2},{2,3},{3,0},{4,5},{5,6},{6,7},{7,4},{8,9},{9,10},{10,1... | collective-permute-start | bytes 1179656 | tf_op jit(solution)/shard_map/ppermute | solution.py:27
  71.4 34.6 %collective-permute-start.16 = (bf16[128,1536]{1,0:T(8,128)(2,1)S(1)}, bf16[128,1536]{1,0:T(8,128)(2,1)S(1)}, u32[]{:S(2)}, u32[]{:S(2)}) collective-permute-start(bf16[128,1536]{1,0:T(8,128)(2,1)S(1)} %get-tuple-element.31), channel_id=1, source_target_pairs={{0,3},{1,0},{2,1},{3,2},{4,7},{5,4},{6,5},{7,6},{8,11},{9,8},{10,9... | collective-permute-start | bytes 1179656 | tf_op jit(solution)/shard_map/ppermute | solution.py:27
  73.0 33.0 %collective-permute-start.17 = (bf16[128,1536]{1,0:T(8,128)(2,1)S(1)}, bf16[128,1536]{1,0:T(8,128)(2,1)S(1)}, u32[]{:S(2)}, u32[]{:S(2)}) collective-permute-start(bf16[128,1536]{1,0:T(8,128)(2,1)S(1)} %get-tuple-element.30), channel_id=1, source_target_pairs={{0,2},{1,3},{2,0},{3,1},{4,6},{5,7},{6,4},{7,5},{8,10},{9,11},{10,... | collective-permute-start | bytes 1179656 | tf_op jit(solution)/shard_map/ppermute | solution.py:27
  77.8 28.3 %collective-permute-start.20 = (bf16[128,1536]{1,0:T(8,128)(2,1)S(1)}, bf16[128,1536]{1,0:T(8,128)(2,1)S(1)}, u32[]{:S(2)}, u32[]{:S(2)}) collective-permute-start(bf16[128,1536]{1,0:T(8,128)(2,1)S(1)} %fusion.48), channel_id=1, source_target_pairs={{0,4},{4,0},{1,5},{5,1},{2,6},{6,2},{3,7},{7,3},{8,12},{12,8},{9,1... | collective-permute-start | bytes 1179656 | tf_op jit(solution)/shard_map/ppermute | solution.py:27
  83.5 15.3 %collective-permute-start.14 = (bf16[128,1536]{1,0:T(8,128)(2,1)S(1)}, bf16[128,1536]{1,0:T(8,128)(2,1)S(1)}, u32[]{:S(2)}, u32[]{:S(2)}) collective-permute-start(bf16[128,1536]{1,0:T(8,128)(2,1)S(1)} %collective-permute-done.6), channel_id=1, source_target_pairs={{0,3},{1,0},{2,1},{3,2},{4,7},{5,4},{6,5},{7,6},{8,11},{9,8},{10,9... | collective-permute-start | bytes 1179656 | tf_op jit(solution)/shard_map/ppermute | solution.py:27
